TPU v7x, 32 devices: a whole 2x2x4 slice. The times are simulated.
32 devices in a mesh: dp: 16 (over z, y, x), fsdp: 2 (over core).
Axes of the slice: x: 2, y: 2, z: 4, core: 2. Of those that a mesh axis runs over, the one named last changes fastest.
Arguments:
- tokens: bfloat16 [16, 512, 1024], P('dp', 'fsdp'), may hold values from -6 to 6
- document_index: int32 [16, 512], P('dp'), may hold values from 0 to 3, never falling along the last dimension, each value on 1 to 256 neighbouring positions
- loss_token_mask: int32 [16, 512], P('dp', 'fsdp'), may hold values 0 or 1
- cotangent: bfloat16 [16, 512, 1024], P('dp', 'fsdp'), may hold values from -6 to 6
- first_gain: bfloat16 [1024], P(('dp', 'fsdp')), may hold values from 0.5 to 1.5
- mixer_in: bfloat16 [1024, 3072], P(('dp', 'fsdp')), may hold values from -0.1875 to 0.1875
- conv_kernel: bfloat16 [3, 1024], P(None, ('dp', 'fsdp')), may hold values from -3.5 to 3.5
- mixer_out: bfloat16 [1024, 1024], P(('dp', 'fsdp')), may hold values from -0.1875 to 0.1875
- second_gain: bfloat16 [1024], P(('dp', 'fsdp')), may hold values from 0.5 to 1.5
- gate_weight: bfloat16 [1024, 4608], P(('dp', 'fsdp')), may hold values from -0.1875 to 0.1875
- up_weight: bfloat16 [1024, 4608], P(('dp', 'fsdp')), may hold values from -0.1875 to 0.1875
- down_weight: bfloat16 [4608, 1024], P(('dp', 'fsdp')), may hold values from -0.09375 to 0.09375
Outputs:
- block_out: bfloat16 [16, 512, 1024], P('dp', 'fsdp')
- input_grad: float32 [16, 512, 1024], P('dp', 'fsdp')
- first_gain_grad: float32 [1024], P(('dp', 'fsdp'))
- mixer_in_grad: float32 [1024, 3072], P(('dp', 'fsdp'))
- conv_kernel_grad: float32 [3, 1024], P(None, ('dp', 'fsdp'))
- mixer_out_grad: float32 [1024, 1024], P(('dp', 'fsdp'))
- second_gain_grad: float32 [1024], P(('dp', 'fsdp'))
- gate_grad: float32 [1024, 4608], P(('dp', 'fsdp'))
- up_grad: float32 [1024, 4608], P(('dp', 'fsdp'))
- down_grad: float32 [4608, 1024], P(('dp', 'fsdp'))
Inputs may be any that keep to these rules, and one draw needn't show every extreme that they name: `document_index`: within a row the ids never fall and each of 0 to 3 forms one run; the longest run holds 256 tokens.
All inputs are finite; a program needn't handle non-finite values. No bound on the sum of `loss_token_mask` on one device may be relied on, other than what follows from the above.
Results may differ from a plain program's by a relative error of at most 0.0086.
Values may be sent and summed in bfloat16 or wider, within the bound.
A program may use at most 256 MiB of HBM per device.

v0:
```python
import jax
import jax.numpy as jnp
from jax import lax
from jax.sharding import PartitionSpec as P

EPSILON = 1e-05


def shifted(value, axis, steps):
    count = lax.axis_size(axis)
    first, last = (max(0, -steps), min(count, count - steps))
    return lax.ppermute(value, axis, [(source, source + steps) for source in range(first, last)])


def product(left_side, right_side):
    return jnp.dot(left_side, right_side, preferred_element_type=jnp.float32)


def over_tokens(left_side, right_side):
    return lax.dot_general(
        left_side, right_side, (((0,), (0,)), ((), ())), preferred_element_type=jnp.float32
    )


def against(left_side, right_side):
    return lax.dot_general(
        left_side, right_side, (((1,), (1,)), ((), ())), preferred_element_type=jnp.float32
    )


def inverse_rms(values):
    return lax.rsqrt(jnp.mean(values * values, axis=1, keepdims=True) + EPSILON)


def norm_back(grad_hidden, gain_row, normed, inverse):
    scaled = grad_hidden * gain_row
    return inverse * (scaled - normed * jnp.mean(scaled * normed, axis=1, keepdims=True))


def per_device(
    tokens,
    document_index,
    loss_token_mask,
    cotangent,
    first_gain,
    mixer_in,
    conv_kernel,
    mixer_out,
    second_gain,
    gate_weight,
    up_weight,
    down_weight,
):
    row_count, seq_here, model_width = tokens.shape
    tok_count = row_count * seq_here
    shards = (
        first_gain,
        mixer_in,
        conv_kernel.T,
        mixer_out,
        second_gain,
        gate_weight,
        up_weight,
        down_weight,
    )
    gathered = (
        lax.all_gather(shards[0], ("dp", "fsdp"), axis=0, tiled=True),
        lax.all_gather(shards[1], ("dp", "fsdp"), axis=0, tiled=True),
        lax.all_gather(shards[2], ("dp", "fsdp"), axis=0, tiled=True),
        lax.all_gather(shards[3], ("dp", "fsdp"), axis=0, tiled=True),
        lax.all_gather(shards[4], ("dp", "fsdp"), axis=0, tiled=True),
        lax.all_gather(shards[5], ("dp", "fsdp"), axis=0, tiled=True),
        lax.all_gather(shards[6], ("dp", "fsdp"), axis=0, tiled=True),
        lax.all_gather(shards[7], ("dp", "fsdp"), axis=0, tiled=True),
    )
    (
        gain_first,
        mixer_in_full,
        kernel_cols,
        mixer_out_full,
        gain_second,
        gate_full,
        up_full,
        down_full,
    ) = gathered
    kernel_full = kernel_cols.T
    offset = lax.axis_index("fsdp") * seq_here
    padded_ids = jnp.pad(document_index, ((0, 0), (2, 2)), constant_values=-1)
    window_ids = lax.dynamic_slice_in_dim(padded_ids, offset, seq_here + 4, 1)
    centre = window_ids[:, 2 : seq_here + 2]
    same_one = (centre == window_ids[:, 1 : seq_here + 1]).astype(jnp.float32)[:, :, None]
    same_two = (centre == window_ids[:, 0:seq_here]).astype(jnp.float32)[:, :, None]
    later_one = (window_ids[:, 3 : seq_here + 3] == centre).astype(jnp.float32)[:, :, None]
    later_two = (window_ids[:, 4 : seq_here + 4] == centre).astype(jnp.float32)[:, :, None]
    stream = tokens.reshape(tok_count, model_width).astype(jnp.float32)
    inverse_one = inverse_rms(stream)
    normed_one = stream * inverse_one
    hidden_one = (normed_one * gain_first.astype(jnp.float32)).astype(jnp.bfloat16)
    projected = product(hidden_one, mixer_in_full)
    before_gate = projected[:, :model_width]
    after_gate = projected[:, model_width : 2 * model_width]
    mixed_in = projected[:, 2 * model_width :]
    conv_input = (before_gate * mixed_in).reshape(row_count, seq_here, model_width)
    earlier = shifted(conv_input[:, seq_here - 2 :, :], "fsdp", 1)
    extended = jnp.concatenate([earlier, conv_input], axis=1)
    back_one = extended[:, 1 : seq_here + 1]
    back_two = extended[:, 0:seq_here]
    kernel_taps = kernel_full.astype(jnp.float32)
    conv_result = (
        kernel_taps[2] * conv_input
        + kernel_taps[1] * same_one * back_one
        + kernel_taps[0] * same_two * back_two
    )
    conv_flat = conv_result.reshape(tok_count, model_width)
    mixer_act = (after_gate * conv_flat).astype(jnp.bfloat16)
    second = stream + product(mixer_act, mixer_out_full)
    inverse_two = inverse_rms(second)
    normed_two = second * inverse_two
    hidden_two = (normed_two * gain_second.astype(jnp.float32)).astype(jnp.bfloat16)
    gate_pre = product(hidden_two, gate_full)
    up_pre = product(hidden_two, up_full)
    gate_sigmoid = jax.nn.sigmoid(gate_pre)
    gate_silu = gate_pre * gate_sigmoid
    inner_act = (gate_silu * up_pre).astype(jnp.bfloat16)
    feed_out = product(inner_act, down_full)
    block_out = (second + feed_out).astype(jnp.bfloat16).reshape(row_count, seq_here, model_width)
    regathered = (
        lax.all_gather(shards[0], ("dp", "fsdp"), axis=0, tiled=True),
        lax.all_gather(shards[1], ("dp", "fsdp"), axis=0, tiled=True),
        lax.all_gather(shards[2], ("dp", "fsdp"), axis=0, tiled=True),
        lax.all_gather(shards[3], ("dp", "fsdp"), axis=0, tiled=True),
        lax.all_gather(shards[4], ("dp", "fsdp"), axis=0, tiled=True),
        lax.all_gather(shards[5], ("dp", "fsdp"), axis=0, tiled=True),
        lax.all_gather(shards[6], ("dp", "fsdp"), axis=0, tiled=True),
        lax.all_gather(shards[7], ("dp", "fsdp"), axis=0, tiled=True),
    )
    (
        gain_first,
        mixer_in_full,
        kernel_cols,
        mixer_out_full,
        gain_second,
        gate_full,
        up_full,
        down_full,
    ) = regathered
    kernel_taps = kernel_cols.T.astype(jnp.float32)
    upstream_low = (cotangent * loss_token_mask.astype(jnp.bfloat16)[:, :, None]).reshape(
        tok_count, model_width
    )
    upstream = upstream_low.astype(jnp.float32)
    down_grad = over_tokens(inner_act, upstream_low)
    grad_inner = against(upstream_low, down_full)
    grad_gate_pre = (
        grad_inner * up_pre * gate_sigmoid * (1.0 + gate_pre * (1.0 - gate_sigmoid))
    ).astype(jnp.bfloat16)
    grad_up_pre = (grad_inner * gate_silu).astype(jnp.bfloat16)
    gate_grad = over_tokens(hidden_two, grad_gate_pre)
    up_grad = over_tokens(hidden_two, grad_up_pre)
    grad_hidden_two = against(grad_gate_pre, gate_full) + against(grad_up_pre, up_full)
    second_gain_grad = jnp.sum(grad_hidden_two * normed_two, axis=0)
    grad_second = upstream + norm_back(
        grad_hidden_two, gain_second.astype(jnp.float32), normed_two, inverse_two
    )
    grad_branch = grad_second.astype(jnp.bfloat16)
    mixer_out_grad = over_tokens(mixer_act, grad_branch)
    grad_mixer = against(grad_branch, mixer_out_full)
    grad_after = grad_mixer * conv_flat
    grad_conv = (grad_mixer * after_gate).reshape(row_count, seq_here, model_width)
    later = shifted(grad_conv[:, 0:2, :], "fsdp", -1)
    ahead = jnp.concatenate([grad_conv, later], axis=1)
    grad_conv_in = (
        kernel_taps[2] * grad_conv
        + kernel_taps[1] * later_one * ahead[:, 1 : seq_here + 1]
        + kernel_taps[0] * later_two * ahead[:, 2 : seq_here + 2]
    )
    kernel_grad_cols = jnp.stack(
        [
            jnp.sum(grad_conv * same_two * back_two, axis=(0, 1)),
            jnp.sum(grad_conv * same_one * back_one, axis=(0, 1)),
            jnp.sum(grad_conv * conv_input, axis=(0, 1)),
        ],
        axis=1,
    )
    grad_conv_flat = grad_conv_in.reshape(tok_count, model_width)
    grad_before = grad_conv_flat * mixed_in
    grad_values = grad_conv_flat * before_gate
    grad_project = jnp.concatenate([grad_before, grad_after, grad_values], axis=1).astype(
        jnp.bfloat16
    )
    mixer_in_grad = over_tokens(hidden_one, grad_project)
    grad_hidden_one = against(grad_project, mixer_in_full)
    first_gain_grad = jnp.sum(grad_hidden_one * normed_one, axis=0)
    input_grad = grad_second + norm_back(
        grad_hidden_one, gain_first.astype(jnp.float32), normed_one, inverse_one
    )
    local_grads = (
        first_gain_grad,
        mixer_in_grad,
        kernel_grad_cols,
        mixer_out_grad,
        second_gain_grad,
        gate_grad,
        up_grad,
        down_grad,
    )
    summed = (
        lax.psum_scatter(local_grads[0], ("dp", "fsdp"), scatter_dimension=0, tiled=True),
        lax.psum_scatter(local_grads[1], ("dp", "fsdp"), scatter_dimension=0, tiled=True),
        lax.psum_scatter(local_grads[2], ("dp", "fsdp"), scatter_dimension=0, tiled=True),
        lax.psum_scatter(local_grads[3], ("dp", "fsdp"), scatter_dimension=0, tiled=True),
        lax.psum_scatter(local_grads[4], ("dp", "fsdp"), scatter_dimension=0, tiled=True),
        lax.psum_scatter(local_grads[5], ("dp", "fsdp"), scatter_dimension=0, tiled=True),
        lax.psum_scatter(local_grads[6], ("dp", "fsdp"), scatter_dimension=0, tiled=True),
        lax.psum_scatter(local_grads[7], ("dp", "fsdp"), scatter_dimension=0, tiled=True),
    )
    all_tokens = tok_count * lax.axis_size("dp") * lax.axis_size("fsdp")
    factor = lax.rsqrt(jnp.asarray(all_tokens, jnp.float32))
    scaled = tuple((item * factor for item in summed))
    return (
        block_out,
        input_grad.reshape(row_count, seq_here, model_width),
        scaled[0],
        scaled[1],
        scaled[2].T,
        scaled[3],
        scaled[4],
        scaled[5],
        scaled[6],
        scaled[7],
    )


def solution(mesh):
    return jax.shard_map(
        per_device,
        mesh=mesh,
        in_specs=(
            P("dp", "fsdp", None),
            P("dp", None),
            P("dp", "fsdp"),
            P("dp", "fsdp", None),
            P(("dp", "fsdp")),
            P(("dp", "fsdp"), None),
            P(None, ("dp", "fsdp")),
            P(("dp", "fsdp"), None),
            P(("dp", "fsdp")),
            P(("dp", "fsdp"), None),
            P(("dp", "fsdp"), None),
            P(("dp", "fsdp"), None),
        ),
        out_specs=(
            P("dp", "fsdp", None),
            P("dp", "fsdp", None),
            P(("dp", "fsdp")),
            P(("dp", "fsdp"), None),
            P(None, ("dp", "fsdp")),
            P(("dp", "fsdp"), None),
            P(("dp", "fsdp")),
            P(("dp", "fsdp"), None),
            P(("dp", "fsdp"), None),
            P(("dp", "fsdp"), None),
        ),
        check_vma=False,
    )
```

profile of v0, /device:TPU:0, one launch (start us, length us, event | category | flops | bytes accessed | tf_op | source)
XLA Modules:
  0.0 1498.6 jit_solution(12101796941470681658)
XLA Ops:
  12.3 42.2 %all-reduce.6 = (bf16[1024]{0:T(1024)(128)(2,1)S(1)}, bf16[1024]{0:T(1024)(128)(2,1)S(1)}) all-reduce(bf16[1024]{0:T(1024)(128)(2,1)S(1)} %dynamic-update-slice, bf16[1024]{0:T(1024)(128)(2,1)S(1)} %dynamic-update-slice.1), channel_id=1, replica_groups=mesh['dp'=16,'fsdp'=2] {'dp','fsdp'}, use_global_device_ids=true, to_apply=%add.1 | all-reduce | flops 2048 | bytes 8192
  54.5 40.9 %all-gather = bf16[32,32,3]{1,2,0:T(4,128)(2,1)S(1)} all-gather(bf16[1,32,3]{1,2,0:T(4,128)(2,1)} %bitcast.110), channel_id=1, replica_groups=mesh['dp'=16,'fsdp'=2] {'dp','fsdp'}, dimensions={0}, use_global_device_ids=true | all-gather | bytes 6336 | tf_op jit(solution)/shard_map/all_gather | solution.py:69
  97.4 4.8 fusion.42
  102.5 2.4 collective-permute-start
  107.2 34.0 %all-gather.9.cloned.1.call-done = bf16[1024,1024]{1,0:T(8,128)(2,1)} async-done(((bf16[32,1024]{1,0:T(8,128)(2,1)}), bf16[1024,1024]{1,0:T(8,128)(2,1)}) %all-gather.9.cloned.1.call-update) | async-done | bytes 2097168 | tf_op jit(solution)/shard_map/all_gather | solution.py:70
  141.2 2.6 multiply_reduce_fusion.3
  145.8 79.2 %all-gather.11.cloned.1.call-done = bf16[1024,4608]{1,0:T(8,128)(2,1)} async-done(((bf16[32,4608]{1,0:T(8,128)(2,1)}), bf16[1024,4608]{1,0:T(8,128)(2,1)}) %all-gather.11.cloned.1.call-update) | async-done | bytes 9437200 | tf_op jit(solution)/shard_map/all_gather | solution.py:72
  225.1 8.7 fusion.50
  233.7 74.8 %all-gather.13.cloned.1.call-done = bf16[1024,4608]{1,0:T(8,128)(2,1)} async-done(((bf16[32,4608]{1,0:T(8,128)(2,1)}), bf16[1024,4608]{1,0:T(8,128)(2,1)}) %all-gather.13.cloned.1.call-update) | async-done | bytes 9437200 | tf_op jit(solution)/shard_map/all_gather | solution.py:73
  308.5 8.7 fusion.51
  317.2 74.7 %all-gather.15.cloned.1.call-done = bf16[4608,1024]{1,0:T(8,128)(2,1)} async-done(((bf16[144,1024]{1,0:T(8,128)(2,1)}), bf16[4608,1024]{1,0:T(8,128)(2,1)}) %all-gather.15.cloned.1.call-update) | async-done | bytes 9437200 | tf_op jit(solution)/shard_map/all_gather | solution.py:74
  391.9 9.8 multiply_convert_fusion
  401.8 6.9 fusion.52
  410.1 2.8 multiply_reduce_fusion
  414.9 2.0 fusion.23
  423.2 4.2 fusion.35
  430.3 6.4 fusion.27
  438.5 7.9 fusion.53
  448.1 7.9 fusion.54
  457.8 7.8 fusion.29
  466.9 8.0 fusion.6
  474.9 4.9 fusion.19
  479.8 39.6 %all-reduce.5 = (f32[1024]{0:T(1024)S(1)}, f32[1024]{0:T(1024)S(1)}) all-reduce(f32[1024]{0:T(1024)S(1)} %get-tuple-element.14, f32[1024]{0:T(1024)S(1)} %get-tuple-element.12), channel_id=2, replica_groups=mesh['dp'=16,'fsdp'=2] {'dp','fsdp'}, use_global_device_ids=true, to_apply=%region_5.6.clone | all-reduce | flops 2048 | bytes 16384
  521.2 34.7 %reduce-scatter.19.cloned.1.call-done = f32[32,3]{1,0:T(8,128)} async-done(((f32[1024,3]{1,0:T(8,128)}), f32[32,3]{1,0:T(8,128)}) %reduce-scatter.19.cloned.1.call-update) | async-done | bytes 400
  557.3 137.8 %reduce-scatter.11.cloned.1.call-done = f32[32,1024]{1,0:T(8,128)} async-done(((f32[1024,1024]{1,0:T(8,128)}), f32[32,1024]{1,0:T(8,128)}) %reduce-scatter.11.cloned.1.call-update) | async-done | bytes 131088 | tf_op jit(solution)/shard_map/reduce_scatter | solution.py:211
  696.7 157.2 %reduce-scatter.9.cloned.1.call-done = f32[32,3072]{1,0:T(8,128)} async-done(((f32[1024,3072]{1,0:T(8,128)}), f32[32,3072]{1,0:T(8,128)}) %reduce-scatter.9.cloned.1.call-update) | async-done | bytes 393232 | tf_op jit(solution)/shard_map/reduce_scatter | solution.py:209
  855.6 210.4 %reduce-scatter.13.cloned.1.call-done = f32[32,4608]{1,0:T(8,128)} async-done(((f32[1024,4608]{1,0:T(8,128)}), f32[32,4608]{1,0:T(8,128)}) %reduce-scatter.13.cloned.1.call-update) | async-done | bytes 589840 | tf_op jit(solution)/shard_map/reduce_scatter | solution.py:213
  1066.0 1.9 broadcast_multiply_fusion.2
  1068.0 210.0 %reduce-scatter.15.cloned.1.call-done = f32[32,4608]{1,0:T(8,128)} async-done(((f32[1024,4608]{1,0:T(8,128)}), f32[32,4608]{1,0:T(8,128)}) %reduce-scatter.15.cloned.1.call-update) | async-done | bytes 589840 | tf_op jit(solution)/shard_map/reduce_scatter | solution.py:214
  1278.0 1.9 broadcast_multiply_fusion.1
  1279.9 210.2 %reduce-scatter.17.cloned.1.call-done = f32[144,1024]{1,0:T(8,128)} async-done(((f32[4608,1024]{1,0:T(8,128)}), f32[144,1024]{1,0:T(8,128)}) %reduce-scatter.17.cloned.1.call-update) | async-done | bytes 589840 | tf_op jit(solution)/shard_map/reduce_scatter | solution.py:215
  1490.1 1.9 broadcast_multiply_fusion
  (113 shorter events, 37.0 us)
Async XLA Ops:
  7.2 90.2 %all-gather.7.cloned.1.call-start = ((), (), s32[]{:S(2)}) async-start(), calls=%async_computation.6 | async-start | bytes 6488064 | tf_op jit(solution)/shard_map/all_gather | solution.py:68
  7.9 133.3 %all-gather.9.cloned.1.call-start = ((), (), s32[]{:S(2)}) async-start(), calls=%async_computation.7 | async-start | bytes 2162688 | tf_op jit(solution)/shard_map/all_gather | solution.py:70
  8.7 216.4 %all-gather.11.cloned.1.call-start = ((), (), s32[]{:S(2)}) async-start(), calls=%async_computation.8 | async-start | bytes 9732096 | tf_op jit(solution)/shard_map/all_gather | solution.py:72
  9.4 299.1 %all-gather.13.cloned.1.call-start = ((), (), s32[]{:S(2)}) async-start(), calls=%async_computation.9 | async-start | bytes 9732096 | tf_op jit(solution)/shard_map/all_gather | solution.py:73
  10.0 381.9 %all-gather.15.cloned.1.call-start = ((), (), s32[]{:S(2)}) async-start(), calls=%async_computation.10 | async-start | bytes 9732096 | tf_op jit(solution)/shard_map/all_gather | solution.py:74
  10.6 545.4 %reduce-scatter.19.cloned.1.call-start = ((), (), s32[]{:S(2)}) async-start(), calls=%async_computation.16 | async-start | bytes 540672
  102.3 2.6 copy-start.26
  102.5 3.1 copy-start.3
  102.5 3.0 collective-permute-start
  401.8 7.0 copy-start.16
  401.8 7.0 copy-start.14
  401.8 8.1 copy-start.5
  401.8 8.4 copy-start.7
  410.1 2.8 copy-start.22
  413.0 1.9 copy-start.11
  414.9 2.0 copy-start
  416.9 3.1 collective-permute-start.1
  422.9 272.2 %reduce-scatter.11.cloned.1.call-start = ((), (), s32[]{:S(2)}) async-start(), calls=%async_computation.12 | async-start | bytes 4325376 | tf_op jit(solution)/shard_map/reduce_scatter | solution.py:211
  427.4 426.5 %reduce-scatter.9.cloned.1.call-start = ((), (), s32[]{:S(2)}) async-start(), calls=%async_computation.11 | async-start | bytes 12976128 | tf_op jit(solution)/shard_map/reduce_scatter | solution.py:209
  427.4 1.9 copy-start.12
  427.4 2.9 copy-start.9
  427.4 2.8 copy-start.24
  436.7 1.8 copy-start.17
  436.7 629.3 %reduce-scatter.13.cloned.1.call-start = ((), (), s32[]{:S(2)}) async-start(), calls=%async_computation.13 | async-start | bytes 19464192 | tf_op jit(solution)/shard_map/reduce_scatter | solution.py:213
  446.5 831.5 %reduce-scatter.15.cloned.1.call-start = ((), (), s32[]{:S(2)}) async-start(), calls=%async_computation.14 | async-start | bytes 19464192 | tf_op jit(solution)/shard_map/reduce_scatter | solution.py:214
  456.1 1.7 copy-start.23
  456.1 1034.0 %reduce-scatter.17.cloned.1.call-start = ((), (), s32[]{:S(2)}) async-start(), calls=%async_computation.15 | async-start | bytes 19464192 | tf_op jit(solution)/shard_map/reduce_scatter | solution.py:215
  466.9 8.0 copy-start.10
  466.9 8.0 copy-start.19
  466.9 8.0 copy-start.21
  466.9 8.0 copy-start.25
  474.9 45.1 %copy-start.1 = (f32[256,1024]{1,0:T(8,128)S(1)}, f32[256,1024]{1,0:T(8,128)}, u32[]{:S(2)}) copy-start(f32[256,1024]{1,0:T(8,128)} %copy-done) | copy-start | bytes 3145732
  (8 other events, 9.5 us)
Sparse Core Ops, SparseCore 0:
  10.9 72.5 all-gather.6
  86.3 54.8 all-gather.8
  144.1 80.8 all-gather.10
  227.8 80.6 all-gather.12
  311.2 80.6 all-gather.14
  423.0 132.8 reduce-scatter.18
  558.3 136.7 reduce-scatter.10
  702.2 151.6 reduce-scatter.8
  860.3 205.7 reduce-scatter.12
  1072.3 205.6 reduce-scatter.14
  1284.4 205.6 reduce-scatter.16
where the time goes:
time: 1500 us
  waiting for transfers between devices  1230 us (82%)
  blocking collectives  123 us (8%)
  matrix products  93.6 us (6%)
  other arithmetic  20.8 us (1%)
    reduce_scatter x1, waiting for transfers between devices, per_device(): lax.psum_scatter(local_grads[5], ('dp', 'fsdp'), scatter_dimension=0, til...  210 us
    reduce_scatter x1, waiting for transfers between devices, per_device(): lax.psum_scatter(local_grads[7], ('dp', 'fsdp'), scatter_dimension=0, til...  210 us
    reduce_scatter x1, waiting for transfers between devices, per_device(): lax.psum_scatter(local_grads[6], ('dp', 'fsdp'), scatter_dimension=0, til...  210 us
    reduce_scatter x1, waiting for transfers between devices, per_device(): lax.psum_scatter(local_grads[1], ('dp', 'fsdp'), scatter_dimension=0, til...  157 us
    reduce_scatter x1, waiting for transfers between devices, per_device(): lax.psum_scatter(local_grads[3], ('dp', 'fsdp'), scatter_dimension=0, til...  138 us
    unnamed x2, blocking collectives  81.7 us
    all_gather x1, waiting for transfers between devices, per_device(): lax.all_gather(shards[5], ('dp', 'fsdp'), axis=0, tiled=True)  79.2 us
    all_gather x1, waiting for transfers between devices, per_device(): lax.all_gather(shards[6], ('dp', 'fsdp'), axis=0, tiled=True)  74.8 us
  transfers between devices with their start and end apart: 13, of which 12 were waited for; matrix products, arithmetic and copies ran while one was open for 6% of the time, Pallas kernels for 0%

commit v1 on v0

v1 whole, which is shorter than its diff:
```python
import functools
import math

import jax
import jax.numpy as jnp
from jax import lax
from jax.experimental import pallas as pl
from jax.experimental.pallas import tpu as pltpu
from jax.sharding import PartitionSpec as P

EPSILON = 1e-05
MESH = pl.DeviceIdType.MESH
F32 = jnp.float32
BF16 = jnp.bfloat16
PLACES = 32


def nn(a, b):
    return jnp.dot(a, b, preferred_element_type=F32)


def nt(a, b):
    return lax.dot_general(a, b, (((1,), (1,)), ((), ())), preferred_element_type=F32)


def tn(a, b):
    return lax.dot_general(a, b, (((0,), (0,)), ((), ())), preferred_element_type=F32)


def kernel(
    fsdp_count,
    copies_of_place,
    factor,
    tokens,
    cotangent,
    document,
    loss_mask,
    gain_one,
    gain_two,
    taps,
    mixer_in,
    mixer_out,
    gate,
    up,
    down,
    block_out,
    input_grad,
    small_out,
    mixer_in_grad,
    mixer_out_grad,
    gate_grad,
    up_grad,
    down_grad,
    small_tile,
    small_all,
    small_grad,
    small_in,
    w_mi,
    w_mo,
    w_gu,
    w_dn,
    mi_stage,
    gu_stage,
    xs,
    flags,
    gs,
    hs,
    proj,
    ubuf,
    conv,
    ys,
    dps,
    x2,
    o_send,
    o_recv,
    pre,
    dm_buf,
    ms,
    dabs,
    acc,
    dhp,
    dh_a,
    dh_b,
    dh_x,
    dh_y,
    dos,
    r_gu_c,
    r_gu_0,
    r_gu_1,
    r_dn_c,
    r_dn_0,
    r_dn_1,
    r_mi_c,
    r_mi_y,
    r_mi_0,
    r_mi_1,
    r_mo_c,
    r_mo_y,
    r_mo_0,
    r_mo_1,
    rows_buf,
    send,
    recv,
    load_sem,
    store_sem,
    small_send,
    small_recv,
    back_send,
    back_recv,
    free_x,
    free_y,
):
    toks, width = tokens.shape
    dkbuf = pre
    rows = mixer_in.shape[0]
    half_width = width // 2
    units = w_dn.shape[0] * w_dn.shape[1] * w_dn.shape[2] * w_dn.shape[3]
    part = units // 3
    half = toks // 2
    step = 32

    dp, fs = lax.axis_index("dp"), lax.axis_index("fsdp")
    number = dp * fsdp_count + fs
    v = lax.div(number, copies_of_place)
    rep = lax.rem(number, copies_of_place)
    c = lax.rem(v, 2)
    x = lax.rem(lax.div(v, 2), 2)
    y = lax.rem(lax.div(v, 4), 2)
    z0 = lax.rem(lax.div(v, 8), 2)
    z1 = lax.div(v, 16)
    p = 2 * y + x
    px = 2 * y + (1 - x)
    py = 2 * (1 - y) + x
    pd = 2 * (1 - y) + (1 - x)

    def dev(place):
        whole = place * copies_of_place + rep
        return (lax.div(whole, fsdp_count), lax.rem(whole, fsdp_count))

    cn = dev(v + (1 - 2 * c))
    xn = dev(v + 2 * (1 - 2 * x))
    yn = dev(v + 4 * (1 - 2 * y))
    dn = dev(v + 2 * (1 - 2 * x) + 4 * (1 - 2 * y))
    z0n = dev(v + 8 * (1 - 2 * z0))
    z1n = dev(v + 16 * (1 - 2 * z1))
    following = (dp, lax.rem(fs + 1, fsdp_count))
    preceding = (dp, lax.rem(fs + fsdp_count - 1, fsdp_count))

    counter = [0]
    started = []

    def remote(src, dst, target):
        at = counter[0]
        counter[0] += 1
        return pltpu.make_async_remote_copy(
            src_ref=src, dst_ref=dst, send_sem=send.at[at], recv_sem=recv.at[at],
            device_id=target, device_id_type=MESH,
        )

    def go(copy):
        copy.start()
        started.append(copy)
        return copy

    def same(ref, target):
        return remote(ref, ref, target)

    def sent(copy):
        copy.wait_send()
        started[:] = [other for other in started if other is not copy]

    barrier = pltpu.get_barrier_semaphore()

    def greet(m, _):
        pl.semaphore_signal(
            barrier, inc=1, device_id=dev(lax.rem(v + m, PLACES)), device_id_type=MESH
        )
        return 0

    lax.fori_loop(1, PLACES, greet, 0)
    pl.semaphore_signal(barrier, inc=1, device_id=following, device_id_type=MESH)
    pl.semaphore_signal(barrier, inc=1, device_id=preceding, device_id_type=MESH)

    load_out = pltpu.make_async_copy(mixer_out, w_mo.at[z1, z0, y, c], load_sem.at[0])
    load_down = pltpu.make_async_copy(down, w_dn.at[z1, z0, c], load_sem.at[1])
    load_cot = pltpu.make_async_copy(cotangent, gs.at[p], load_sem.at[2])
    load_out.start()
    load_down.start()
    load_cot.start()

    lane = lax.broadcasted_iota(jnp.int32, (1, 128), 1)
    mine = lax.div(lane, 32) == lax.rem(v, 4)
    small_tile[...] = jnp.zeros_like(small_tile)

    def spread(values):
        wide = jnp.concatenate([values.astype(F32)] * 4, axis=1)
        return jnp.where(mine, wide, 0.0)

    small_tile[0:1, :] = spread(gain_one[...])
    small_tile[1:2, :] = spread(gain_two[...])
    small_tile[2:5, :] = spread(taps[...])

    lanes128 = lax.broadcasted_iota(jnp.int32, (rows, 128), 1)
    low = lanes128 < 64
    for b in range(3):
        for q in range(width // 256):
            at = b * width + 256 * q
            even = mixer_in[:, at : at + 128].astype(F32)
            odd = mixer_in[:, at + 128 : at + 256].astype(F32)
            to = b * half_width + 128 * q
            mi_stage[0, :, to : to + 128] = jnp.where(low, even, pltpu.roll(odd, 64, 1)).astype(BF16)
            mi_stage[1, :, to : to + 128] = jnp.where(low, pltpu.roll(even, 64, 1), odd).astype(BF16)
    w_mi[z1, z0, y, x, c] = mi_stage[x]
    small_all[v] = small_tile[...]

    pl.semaphore_wait(barrier, PLACES + 1)

    mi_swap = go(remote(mi_stage.at[1 - x], w_mi.at[z1, z0, y, x, c], xn))

    def small_copy(src, dst, m, sems=(small_send, small_recv)):
        return pltpu.make_async_remote_copy(
            src_ref=src, dst_ref=dst, send_sem=sems[0].at[m], recv_sem=sems[1].at[m],
            device_id=dev(lax.rem(v + m, PLACES)), device_id_type=MESH,
        )

    def small_start(m, _):
        small_copy(small_tile, small_all.at[v], m).start()
        return 0

    lax.fori_loop(1, PLACES, small_start, 0)
    tok_swap = go(remote(tokens, xs.at[x], xn))

    def mo_at(a, b, yy, cc):
        return w_mo.at[a, b, yy, cc]

    def mi_at(a, b, yy, cc):
        return w_mi.at[a, b, yy, :, cc]

    def mix_gather(at):
        return dict(
            s1=same(at(z1, z0, y, c), z1n),
            s2=same(at(z1, z0, y, c), z0n),
            s3=same(at(1 - z1, z0, y, c), z0n),
            y0=same(at(z1, z0, y, c), yn),
            y1=same(at(1 - z1, z0, y, c), yn),
            y2=same(at(z1, 1 - z0, y, c), yn),
            y3=same(at(1 - z1, 1 - z0, y, c), yn),
        )

    mo_g, mi_g = mix_gather(mo_at), mix_gather(mi_at)
    load_out.wait()
    for name in ("s1", "s2", "y0"):
        go(mo_g[name])
    mi_swap.wait_recv()
    for name in ("s1", "s2", "y0"):
        go(mi_g[name])

    offset = fs * toks
    ids = document[...].astype(F32) + 1.0
    mask_row = loss_mask[...].astype(F32)
    id_lane = lax.broadcasted_iota(jnp.int32, (step, ids.shape[1]), 1)
    id_row = lax.broadcasted_iota(jnp.int32, (step, ids.shape[1]), 0)
    ma_lane = lax.broadcasted_iota(jnp.int32, (step, toks), 1)
    ma_row = lax.broadcasted_iota(jnp.int32, (step, toks), 0)
    fl_lane = lax.broadcasted_iota(jnp.int32, (step, 128), 1)

    def flag_rows(i, _):
        base = i * step
        at = pl.ds(pl.multiple_of(base, step), step)

        def column(shift):
            hit = id_lane == id_row + (offset + base + shift)
            return jnp.sum(jnp.where(hit, ids, 0.0), axis=1, keepdims=True)

        centre = column(0)
        tile = jnp.zeros((step, 128), F32)
        for k, shift in enumerate((-1, -2, 1, 2)):
            tile = jnp.where(
                jnp.logical_and(fl_lane == k, column(shift) == centre), 1.0, tile
            )
        flags[x, at, :] = tile.astype(BF16)
        keep = jnp.sum(
            jnp.where(ma_lane == ma_row + base, mask_row, 0.0), axis=1, keepdims=True
        )
        gs[p, at, :] = (gs[p, at, :].astype(F32) * keep).astype(BF16)
        return 0

    load_cot.wait()
    lax.fori_loop(0, toks // step, flag_rows, 0)
    flag_swap = go(same(flags.at[x], xn))
    xs[x] = tokens[...]

    run = units // 4
    def pick(ref, at_p):
        whole = ref[...].astype(F32)
        return jnp.concatenate(
            [whole[:, run * (4 * z + at_p) : run * (4 * z + at_p) + run] for z in range(4)], axis=1
        ).astype(BF16)

    for at_p in range(4):
        picked_gate, picked_up = pick(gate, at_p), pick(up, at_p)
        for j in range(3):
            gu_stage[at_p, j, :, 0:part] = picked_gate[:, j * part : j * part + part]
            gu_stage[at_p, j, :, part:] = picked_up[:, j * part : j * part + part]
    for j in range(3):
        w_gu[j, z1, z0, p, c] = gu_stage[p, j]

    def forward(g, arrived, names):
        g[arrived].wait_recv()
        for name in names:
            go(g[name])

    for g in (mo_g, mi_g):
        forward(g, "s1", ("s3", "y1"))
        forward(g, "s2", ("y2",))
        forward(g, "s3", ("y3",))

    gu_swap = [
        go(remote(gu_stage.at[px], w_gu.at[:, z1, z0, p, c], xn)),
        go(remote(gu_stage.at[py], w_gu.at[:, z1, z0, p, c], yn)),
        go(remote(gu_stage.at[pd], w_gu.at[:, z1, z0, p, c], dn)),
    ]

    def z_gather(at):
        return dict(
            s1=same(at(z1, z0, c), z1n),
            s2=same(at(z1, z0, c), z0n),
            s3=same(at(1 - z1, z0, c), z0n),
            core=same(at(slice(None), slice(None), c), cn),
        )

    dn_g = z_gather(lambda a, b, cc: w_dn.at[a, b, cc])
    gu_g = [z_gather(lambda a, b, cc, j=j: w_gu.at[j, a, b, :, cc]) for j in range(3)]
    load_down.wait()
    go(dn_g["s1"])
    go(dn_g["s2"])

    def plane_gather(buf):
        lo, hi = pl.ds(0, half), pl.ds(half, half)
        g = dict(
            x0=same(buf.at[p, lo], xn),
            y1=same(buf.at[p, hi], yn),
            x1=same(buf.at[p, hi], xn),
            y0=same(buf.at[p, lo], yn),
            fx=same(buf.at[px, lo], yn),
            fy=same(buf.at[py, hi], xn),
        )
        for name in ("x0", "y1", "x1", "y0"):
            go(g[name])
        return g

    def plane_forward(g):
        forward(g, "x0", ("fx",))
        forward(g, "y1", ("fy",))

    gs_g = plane_gather(gs)

    def small_wait(m, _):
        copy = small_copy(small_tile, small_all.at[v], m)
        copy.wait()
        return 0

    lax.fori_loop(1, PLACES, small_wait, 0)
    natural = []
    for q in range(8):
        natural.append(
            small_all[4 * q] + small_all[4 * q + 1] + small_all[4 * q + 2] + small_all[4 * q + 3]
        )
    for q in range(8):
        rows_buf[:, 128 * q : 128 * q + 128] = natural[q]
    low8 = lax.broadcasted_iota(jnp.int32, (8, 128), 1) < 64
    is_one = x == 1
    for q in range(4):
        even, odd = natural[2 * q], natural[2 * q + 1]
        first = jnp.where(low8, even, pltpu.roll(odd, 64, 1))
        second = jnp.where(low8, pltpu.roll(even, 64, 1), odd)
        rows_buf[:, width + 128 * q : width + 128 * q + 128] = jnp.where(is_one, second, first)
    g1 = rows_buf[0:1, 0:width]
    g2 = rows_buf[1:2, 0:width]
    tap0 = rows_buf[2:3, width : width + half_width]
    tap1 = rows_buf[3:4, width : width + half_width]
    tap2 = rows_buf[4:5, width : width + half_width]

    def inverse_rms(values):
        return lax.rsqrt(jnp.mean(values * values, axis=1, keepdims=True) + EPSILON)

    def loop(count, body):
        def wrapped(i, _):
            body(pl.ds(pl.multiple_of(i * step, step), step))
            return 0

        lax.fori_loop(0, count // step, wrapped, 0)

    def hidden_one(s):
        def body(at):
            values = xs[s, at, :].astype(F32)
            xs[s, at, :] = (values * inverse_rms(values) * g1).astype(BF16)

        loop(toks, body)

    hidden_one(x)
    tok_swap.wait_recv()
    hidden_one(1 - x)

    for g in (mo_g, mi_g):
        for name in ("y0", "y1", "y2", "y3"):
            g[name].wait_recv()
    every = slice(None)
    mo_core = go(same(w_mo.at[:, :, :, c], cn))
    mi_core = go(same(w_mi.at[:, :, :, :, c], cn))
    mi_core.wait_recv()
    h1 = xs[...].reshape(2 * toks, width)
    wide = 3 * half_width
    proj[...] = nn(h1, w_mi[...].reshape(width, wide)).reshape(2, toks, wide)

    for s in range(2):
        def body(at, s=s):
            ubuf[s, pl.ds(pl.multiple_of(at.start + 8, 8), step), :] = (
                proj[s, at, 0:half_width] * proj[s, at, 2 * half_width :]
            )

        loop(toks, body)
    halo = go(remote(ubuf.at[:, pl.ds(toks, 8), :], ubuf.at[:, pl.ds(0, 8), :], following))
    flag_swap.wait_recv()
    halo.wait_recv()
    for s in range(2):
        for i in range(toks // step):
            a = i * step
            fl = flags[s, a : a + step, :].astype(F32)
            value = (
                tap2 * ubuf[s, a + 8 : a + 8 + step, :]
                + tap1 * (fl[:, 0:1] * ubuf[s, a + 7 : a + 7 + step, :])
                + tap0 * (fl[:, 1:2] * ubuf[s, a + 6 : a + 6 + step, :])
            )
            conv[s, a : a + step, :] = value
            ys[s, a : a + step, :] = (
                proj[s, a : a + step, half_width : 2 * half_width] * value
            ).astype(BF16)
    mo_core.wait_recv()
    mo_flat = w_mo[...].reshape(half_width, width)
    o_send[...] = nn(ys[1 - x], mo_flat).astype(BF16)
    o_swap = go(remote(o_send, o_recv, xn))
    x2[...] = nn(ys[x], mo_flat)

    def z_forward(g):
        forward(g, "s1", ("s3",))

    def z_core(g):
        g["s2"].wait_recv()
        g["s3"].wait_recv()
        go(g["core"])

    z_forward(dn_g)
    plane_forward(gs_g)
    for copy in gu_swap:
        copy.wait_recv()
        sent(copy)
    sent(mi_swap)
    go(gu_g[0]["s1"])
    go(gu_g[0]["s2"])
    z_core(dn_g)

    o_swap.wait_recv()

    def second_body(at):
        values = tokens[at, :].astype(F32) + x2[at, :] + o_recv[at, :].astype(F32)
        x2[at, :] = values
        hs[p, at, :] = (values * inverse_rms(values) * g2).astype(BF16)

    loop(toks, second_body)
    hs_g = plane_gather(hs)
    z_forward(gu_g[0])
    go(gu_g[1]["s1"])
    go(gu_g[1]["s2"])
    plane_forward(hs_g)
    z_core(gu_g[0])
    z_forward(gu_g[1])
    go(gu_g[2]["s1"])
    go(gu_g[2]["s2"])

    ya, yb = 2 * y, 2 * (1 - y)

    def plane_pair(g, names):
        for name in names:
            g[name].wait_recv()

    def pair_rows(ref, base):
        return ref[pl.ds(base, 2)].reshape(2 * toks, width)

    def feed(j, base):
        w = w_gu[j].reshape(width, 2 * part)
        pre[:, 0:toks, :] = nn(pair_rows(hs, base), w).reshape(2, toks, 2 * part)
        down_rows = w_dn[...].reshape(units, width)[j * part : j * part + part]
        dm_buf[...] = nt(pair_rows(gs, base), down_rows)

        def body(i, _):
            at = pl.ds(pl.multiple_of(i * step, step), step)
            slot = base + lax.div(i, toks // step)
            inner = pl.ds(pl.multiple_of(lax.rem(i, toks // step) * step, step), step)
            which = lax.div(i, toks // step)
            a = pre[which, inner, 0:part]
            b = pre[which, inner, part:]
            d = dm_buf[at, :]
            sg = jax.nn.sigmoid(a)
            silu = a * sg
            ms[slot, inner, j * part : j * part + part] = (silu * b).astype(BF16)
            dabs[j, slot, inner, 0:part] = (d * b * sg * (1.0 + a * (1.0 - sg))).astype(BF16)
            dabs[j, slot, inner, part:] = (d * silu).astype(BF16)
            return 0

        lax.fori_loop(0, 2 * toks // step, body, 0)
        back = nt(dabs[j, pl.ds(base, 2)].reshape(2 * toks, 2 * part), w)
        back = back.reshape(2, toks, width)
        if j == 0:
            acc[pl.ds(base, 2)] = back
        elif j == 1:
            acc[pl.ds(base, 2)] += back
        else:
            total = acc[pl.ds(base, 2)] + back
            acc[pl.ds(base, 2)] = total
            dhp[pl.ds(base, 2)] = total.astype(BF16)

    def gu_weight_grad(j):
        w_gu[j] = (
            tn(hs[...].reshape(4 * toks, width), dabs[j].reshape(4 * toks, 2 * part))
            .astype(BF16)
            .reshape(w_gu.shape[1:])
        )

    def plane_scatter(buf, r_a, r_b, r_x, r_y):
        lo, hi = pl.ds(0, half), pl.ds(half, half)
        return dict(
            a=remote(buf.at[pd, lo], r_a, xn),
            b=remote(buf.at[pd, hi], r_b, yn),
            x0=remote(buf.at[px, lo], r_x.at[lo], xn),
            y1=remote(buf.at[py, hi], r_y.at[hi], yn),
            x1=remote(buf.at[px, hi], r_x.at[hi], xn),
            y0=remote(buf.at[py, lo], r_y.at[lo], yn),
        )

    def add_rows(buf, slot, start, other):
        def body(at):
            into = pl.ds(pl.multiple_of(at.start + start, step), step)
            buf[slot, into, :] = (
                buf[slot, into, :].astype(F32) + other[at, :].astype(F32)
            ).astype(BF16)

        loop(half, body)

    def scatter_rest(g, buf, r_a, r_b):
        g["b"].wait_recv()
        add_rows(buf, px, half, r_b)
        go(g["x1"])
        g["a"].wait_recv()
        add_rows(buf, py, 0, r_a)
        go(g["y0"])

    dn_g["core"].wait_recv()
    plane_pair(gs_g, ("x1",))
    plane_pair(hs_g, ("x1",))
    gu_g[0]["core"].wait_recv()
    feed(0, ya)
    plane_pair(gs_g, ("y0", "fx", "fy"))
    plane_pair(hs_g, ("y0", "fx", "fy"))
    feed(0, yb)

    def z_reduce(at, r_c, r_0, r_1):
        return dict(
            core=remote(at(every, every, 1 - c), r_c, cn),
            z0=remote(at(every, 1 - z0, c), r_0, z0n),
            z1=remote(at(1 - z1, z0, c), r_1, z1n),
        )

    gu_r = [
        z_reduce(lambda a, b, cc, j=j: w_gu.at[j, a, b, :, cc], r_gu_c.at[j % 2], r_gu_0.at[j], r_gu_1.at[j])
        for j in range(3)
    ]
    dn_r = z_reduce(lambda a, b, cc: w_dn.at[a, b, cc], r_dn_c, r_dn_0, r_dn_1)

    def plus(one, two):
        return (one.astype(F32) + two.astype(F32)).astype(BF16)

    def gu_after_core(j):
        gu_r[j]["core"].wait_recv()
        for a in range(2):
            for b in range(2):
                w_gu[j, a, b, :, c] = plus(w_gu[j, a, b, :, c], r_gu_c[j % 2, a, b])
        go(gu_r[j]["z0"])

    def gu_after_z0(j):
        gu_r[j]["z0"].wait_recv()
        for a in range(2):
            w_gu[j, a, z0, :, c] = plus(w_gu[j, a, z0, :, c], r_gu_0[j, a])
        go(gu_r[j]["z1"])

    def gu_after_z1(j):
        gu_r[j]["z1"].wait_recv()
        w_gu[j, z1, z0, :, c] = plus(w_gu[j, z1, z0, :, c], r_gu_1[j])
        gu_stage[p, j] = w_gu[j, z1, z0, p, c]
        return [
            go(remote(w_gu.at[j, z1, z0, px, c], gu_stage.at[p, j], xn)),
            go(remote(w_gu.at[j, z1, z0, py, c], gu_stage.at[p, j], yn)),
            go(remote(w_gu.at[j, z1, z0, pd, c], gu_stage.at[p, j], dn)),
        ]

    def gathered(g):
        for name in ("s1", "s2", "s3", "core"):
            sent(g[name])

    gathered(gu_g[0])
    gu_weight_grad(0)
    go(gu_r[0]["core"])
    z_core(gu_g[1])
    z_forward(gu_g[2])
    gu_after_core(0)
    gu_g[1]["core"].wait_recv()
    feed(1, ya)
    feed(1, yb)
    gathered(gu_g[1])
    gu_weight_grad(1)
    go(gu_r[1]["core"])
    z_core(gu_g[2])
    gu_after_core(1)
    gu_g[2]["core"].wait_recv()
    feed(2, yb)
    dh_g = plane_scatter(dhp, dh_a, dh_b, dh_x, dh_y)
    go(dh_g["a"])
    go(dh_g["b"])
    go(dh_g["y1"])
    feed(2, ya)
    go(dh_g["x0"])
    gathered(gu_g[2])
    gu_weight_grad(2)
    go(gu_r[2]["core"])
    scatter_rest(dh_g, dhp, dh_a, dh_b)
    gu_after_z0(0)
    gu_after_core(2)

    for name in ("x0", "x1", "y0", "y1", "fx", "fy"):
        sent(hs_g[name])
    dn_flat = w_dn[...].reshape(units, width)
    for base in (ya, yb):
        m = ms[pl.ds(base, 2)].reshape(2 * toks, units)
        hs[pl.ds(base, 2)] = nn(m, dn_flat).astype(BF16).reshape(2, toks, width)
    gathered(dn_g)
    w_dn[...] = (
        tn(ms[...].reshape(4 * toks, units), gs[...].reshape(4 * toks, width))
        .astype(BF16)
        .reshape(w_dn.shape)
    )
    go(dn_r["core"])
    gu_after_z0(1)

    for name in ("x0", "x1", "y0", "y1"):
        dh_g[name].wait_recv()
    small_grad[...] = jnp.zeros_like(small_grad)

    def norm_two(at):
        dh = acc[p, at, :] + dh_x[at, :].astype(F32) + dh_y[at, :].astype(F32)
        values = x2[at, :]
        inverse = inverse_rms(values)
        normed = values * inverse
        small_grad[1:2, :] += jnp.sum(dh * normed, axis=0, keepdims=True)
        q = dh * g2
        grad = gs[p, at, :].astype(F32) + inverse * (
            q - normed * jnp.mean(q * normed, axis=1, keepdims=True)
        )
        input_grad[at, :] = grad
        dos[x, at, :] = grad.astype(BF16)

    loop(toks, norm_two)
    do_swap = go(same(dos.at[x], xn))
    lo, hi = pl.ds(0, half), pl.ds(half, half)
    ou_g = plane_scatter(hs, dhp.at[py, lo], dhp.at[px, hi], dhp.at[p], dhp.at[p])
    for copy in dh_g.values():
        sent(copy)
    pl.semaphore_signal(free_x, inc=1, device_id=xn, device_id_type=MESH)
    pl.semaphore_signal(free_y, inc=1, device_id=yn, device_id_type=MESH)
    pl.semaphore_wait(free_x, 1)
    pl.semaphore_wait(free_y, 1)
    for name in ("a", "b", "x0", "y1"):
        go(ou_g[name])

    mo_flat = w_mo[...].reshape(half_width, width)

    def split_dy(s):
        def body(at):
            dy = dkbuf[s, at, 0:half_width]
            dps[s, at, half_width : 2 * half_width] = (dy * conv[s, at, :]).astype(BF16)
            dkbuf[s, at, 0:half_width] = dy * proj[s, at, half_width : 2 * half_width]

        loop(toks, body)

    dkbuf[x, 0:toks, 0:half_width] = nt(dos[x], mo_flat)
    split_dy(x)
    dn_r["core"].wait_recv()
    for a in range(2):
        for b in range(2):
            w_dn[a, b, c] = plus(w_dn[a, b, c], r_dn_c[a, b])
    go(dn_r["z0"])
    do_swap.wait_recv()
    dkbuf[1 - x, 0:toks, 0:half_width] = nt(dos[1 - x], mo_flat)
    split_dy(1 - x)
    dk_halo = go(
        remote(
            dkbuf.at[:, pl.ds(0, 8), pl.ds(0, half_width)],
            dkbuf.at[:, pl.ds(toks, 8), pl.ds(0, half_width)],
            preceding,
        )
    )
    for name in ("s1", "s2", "s3", "y0", "y1", "y2", "y3"):
        sent(mo_g[name])
        sent(mi_g[name])
    sent(mo_core)
    sent(mi_core)
    w_mo[...] = (
        tn(ys[...].reshape(2 * toks, half_width), dos[...].reshape(2 * toks, width))
        .astype(BF16)
        .reshape(w_mo.shape)
    )

    def mix_reduce(at, r_c, r_y, r_0, r_1):
        return dict(
            core=remote(at(every, every, every, 1 - c), r_c, cn),
            y3=remote(at(1 - z1, 1 - z0, 1 - y, c), r_y.at[1 - z1, 1 - z0], yn),
            y2=remote(at(z1, 1 - z0, 1 - y, c), r_y.at[z1, 1 - z0], yn),
            y1=remote(at(1 - z1, z0, 1 - y, c), r_y.at[1 - z1, z0], yn),
            y0=remote(at(z1, z0, 1 - y, c), r_y.at[z1, z0], yn),
            s3=remote(at(1 - z1, 1 - z0, y, c), r_0.at[1 - z1], z0n),
            s2=remote(at(z1, 1 - z0, y, c), r_0.at[z1], z0n),
            s1=remote(at(1 - z1, z0, y, c), r_1, z1n),
        )

    mo_r = mix_reduce(mo_at, r_mo_c, r_mo_y, r_mo_0, r_mo_1)
    mi_r = mix_reduce(mi_at, r_mi_c, r_mi_y, r_mi_0, r_mi_1)
    go(mo_r["core"])
    dk_halo.wait_recv()
    ek = [jnp.zeros((1, half_width), F32) for _ in range(3)]
    for s in range(2):
        for i in range(toks // step):
            a = i * step
            fl = flags[s, a : a + step, :].astype(F32)
            dk = dkbuf[s, a : a + step, 0:half_width]
            ek[2] += jnp.sum(dk * ubuf[s, a + 8 : a + 8 + step, :], axis=0, keepdims=True)
            ek[1] += jnp.sum(
                dk * (fl[:, 0:1] * ubuf[s, a + 7 : a + 7 + step, :]), axis=0, keepdims=True
            )
            ek[0] += jnp.sum(
                dk * (fl[:, 1:2] * ubuf[s, a + 6 : a + 6 + step, :]), axis=0, keepdims=True
            )
            du = (
                tap2 * dk
                + tap1 * (fl[:, 2:3] * dkbuf[s, a + 1 : a + 1 + step, 0:half_width])
                + tap0 * (fl[:, 3:4] * dkbuf[s, a + 2 : a + 2 + step, 0:half_width])
            )
            dps[s, a : a + step, 0:half_width] = (
                du * proj[s, a : a + step, 2 * half_width :]
            ).astype(BF16)
            dps[s, a : a + step, 2 * half_width :] = (
                du * proj[s, a : a + step, 0:half_width]
            ).astype(BF16)
    for k in range(3):
        for q in range(4):
            chunk = jnp.broadcast_to(ek[k][:, 128 * q : 128 * q + 128], (8, 128))
            turned = pltpu.roll(chunk, 64, 1)
            even = jnp.where(is_one, jnp.where(low8, 0.0, turned), jnp.where(low8, chunk, 0.0))
            odd = jnp.where(is_one, jnp.where(low8, 0.0, chunk), jnp.where(low8, turned, 0.0))
            small_grad[2 + k : 3 + k, 256 * q : 256 * q + 128] = even[0:1]
            small_grad[2 + k : 3 + k, 256 * q + 128 : 256 * q + 256] = odd[0:1]

    mi_flat = w_mi[...].reshape(width, wide)
    sent(o_swap)
    o_send[...] = nt(dps[1 - x], mi_flat).astype(BF16)
    dh1_swap = go(remote(o_send, o_recv, xn))
    acc[p] = nt(dps[x], mi_flat)
    w_mi[...] = (
        tn(xs[...].reshape(2 * toks, width), dps[...].reshape(2 * toks, wide))
        .astype(BF16)
        .reshape(w_mi.shape)
    )
    go(mi_r["core"])
    scatter_rest(ou_g, hs, dhp.at[pd, lo], dhp.at[pd, hi])
    gu_after_z0(2)

    def mix_core(w, r_c, g, with_x):
        g["core"].wait_recv()
        for a in range(2):
            for b in range(2):
                for yy in range(2):
                    if with_x:
                        w[a, b, yy, :, c] = plus(w[a, b, yy, :, c], r_c[a, b, yy])
                    else:
                        w[a, b, yy, c] = plus(w[a, b, yy, c], r_c[a, b, yy])
        for name in ("y3", "y2", "y1", "y0"):
            go(g[name])

    mix_core(w_mo, r_mo_c, mo_r, False)
    mix_core(w_mi, r_mi_c, mi_r, True)

    dn_r["z0"].wait_recv()
    for a in range(2):
        w_dn[a, z0, c] = plus(w_dn[a, z0, c], r_dn_0[a])
    go(dn_r["z1"])

    dh1_swap.wait_recv()

    def norm_one(at):
        dh = acc[p, at, :] + o_recv[at, :].astype(F32)
        values = tokens[at, :].astype(F32)
        inverse = inverse_rms(values)
        normed = values * inverse
        small_grad[0:1, :] += jnp.sum(dh * normed, axis=0, keepdims=True)
        q = dh * g1
        input_grad[at, :] = input_grad[at, :] + inverse * (
            q - normed * jnp.mean(q * normed, axis=1, keepdims=True)
        )

    loop(toks, norm_one)

    for q in range(8):
        small_in[PLACES + q] = small_grad[:, 128 * q : 128 * q + 128]

    def small_back(m):
        target = lax.rem(v + m, PLACES)
        source = small_in.at[PLACES + lax.div(target, 4)]
        return small_copy(source, small_in.at[v], m, (back_send, back_recv))

    def small_back_start(m, _):
        small_back(m).start()
        return 0

    lax.fori_loop(1, PLACES, small_back_start, 0)
    small_in[v] = small_in[PLACES + lax.div(v, 4)]

    gu_back = gu_after_z1(0)
    gu_back += gu_after_z1(1)

    def mo_idx(a, b):
        return (a, b, y, c)

    def mi_idx(a, b):
        return (a, b, y, every, c)

    def mix_rest(w, idx, g, r_y, r_0, r_1):
        def add(a, b, other):
            w[idx(a, b)] = plus(w[idx(a, b)], other)

        g["y3"].wait_recv()
        add(1 - z1, 1 - z0, r_y[1 - z1, 1 - z0])
        go(g["s3"])
        g["y2"].wait_recv()
        add(z1, 1 - z0, r_y[z1, 1 - z0])
        go(g["s2"])
        g["y1"].wait_recv()
        add(1 - z1, z0, r_y[1 - z1, z0])
        g["s3"].wait_recv()
        add(1 - z1, z0, r_0[1 - z1])
        go(g["s1"])
        g["y0"].wait_recv()
        add(z1, z0, r_y[z1, z0])
        g["s2"].wait_recv()
        add(z1, z0, r_0[z1])

    mix_rest(w_mo, mo_idx, mo_r, r_mo_y, r_mo_0, r_mo_1)
    mix_rest(w_mi, mi_idx, mi_r, r_mi_y, r_mi_0, r_mi_1)
    gu_back += gu_after_z1(2)

    for name in ("x0", "x1", "y0", "y1"):
        ou_g[name].wait_recv()

    def out_body(at):
        o_send[at, :] = (
            x2[at, :]
            + hs[p, at, :].astype(F32)
            + dhp[px, at, :].astype(F32)
            + dhp[py, at, :].astype(F32)
        ).astype(BF16)

    sent(dh1_swap)
    loop(toks, out_body)

    stores = []

    def store(src, dst):
        copy = pltpu.make_async_copy(src, dst, store_sem.at[len(stores)])
        copy.start()
        stores.append(copy)

    store(o_send, block_out)
    down_rows = w_dn.shape[3]
    dn_r["z1"].wait_recv()
    acc[3, 0:down_rows] = (w_dn[z1, z0, c].astype(F32) + r_dn_1[...].astype(F32)) * factor
    store(acc.at[3, pl.ds(0, down_rows)], down_grad)
    mo_r["s1"].wait_recv()
    acc[2, 96 : 96 + rows] = (w_mo[z1, z0, y, c].astype(F32) + r_mo_1[...].astype(F32)) * factor
    store(acc.at[2, pl.ds(96, rows)], mixer_out_grad)
    mi_r["s1"].wait_recv()
    w_mi[z1, z0, y, :, c] = plus(w_mi[z1, z0, y, :, c], r_mi_1[...])
    mi_stage[x] = w_mi[z1, z0, y, x, c]
    mi_back = go(remote(w_mi.at[z1, z0, y, 1 - x, c], mi_stage.at[x], xn))

    for copy in gu_back:
        copy.wait_recv()
    for slot, (ref, start) in enumerate(((gate_grad, 0), (up_grad, part))):
        pieces = []
        for at_p in range(4):
            whole = jnp.concatenate(
                [gu_stage[at_p, j, :, start : start + part] for j in range(3)], axis=1
            ).astype(F32)
            pieces.append(whole * factor)
        whole = jnp.concatenate(
            [pieces[q % 4][:, run * (q // 4) : run * (q // 4) + run] for q in range(16)], axis=1
        )
        for k, first in enumerate(range(0, whole.shape[1], width)):
            count = min(width, whole.shape[1] - first)
            acc[slot, k * rows : k * rows + rows, 0:count] = whole[:, first : first + count]
            store(
                acc.at[slot, pl.ds(k * rows, rows), pl.ds(0, count)],
                ref.at[:, pl.ds(first, count)],
            )
    mi_back.wait_recv()
    for b in range(3):
        for q in range(width // 256):
            at = b * half_width + 128 * q
            first = mi_stage[0, :, at : at + 128].astype(F32) * factor
            second = mi_stage[1, :, at : at + 128].astype(F32) * factor
            to, block = 256 * q, pl.ds(b * rows, rows)
            acc[2, block, to : to + 128] = jnp.where(low, first, pltpu.roll(second, 64, 1))
            acc[2, block, to + 128 : to + 256] = jnp.where(low, pltpu.roll(first, 64, 1), second)
        store(acc.at[2, pl.ds(b * rows, rows)], mixer_in_grad.at[:, pl.ds(b * width, width)])

    def small_back_wait(m, _):
        small_back(m).wait()
        return 0

    lax.fori_loop(1, PLACES, small_back_wait, 0)
    total = small_in[0]
    for q in range(1, PLACES):
        total = total + small_in[q]
    total = total * factor
    small_out[...] = total

    for copy in stores:
        copy.wait()
    for copy in list(started):
        sent(copy)


COPIES = 160


def per_device(
    fsdp_count,
    device_count,
    tokens,
    document_index,
    loss_token_mask,
    cotangent,
    first_gain,
    mixer_in,
    conv_kernel,
    mixer_out,
    second_gain,
    gate_weight,
    up_weight,
    down_weight,
):
    row_count, seq_here, width = tokens.shape
    toks = row_count * seq_here
    spare = device_count // PLACES
    groups = [[place * spare + k for k in range(spare)] for place in range(PLACES)]
    axes = ("dp", "fsdp")

    def joined(shard, axis=0):
        if spare == 1:
            return shard
        return lax.all_gather(shard, axes, axis=axis, tiled=True, axis_index_groups=groups)

    first_gain, second_gain = joined(first_gain), joined(second_gain)
    conv_kernel = joined(conv_kernel, 1)
    mixer_in, mixer_out = joined(mixer_in), joined(mixer_out)
    gate_weight, up_weight, down_weight = joined(gate_weight), joined(up_weight), joined(down_weight)
    rows = mixer_in.shape[0]
    down_rows = down_weight.shape[0]
    ff = gate_weight.shape[1]
    part = ff // 12
    half_width = width // 2
    wide = 3 * half_width
    factor = 1.0 / math.sqrt(toks * device_count)

    def vm(shape, dtype=BF16):
        return pltpu.VMEM(shape, dtype)

    half = toks // 2
    scratch = [
        vm((8, 128), F32),
        vm((PLACES, 8, 128), F32),
        vm((8, width), F32),
        vm((PLACES + 8, 8, 128), F32),
        vm((2, 2, 2, 2, 2, rows, wide)),
        vm((2, 2, 2, 2, rows, width)),
        vm((3, 2, 2, 4, 2, rows, 2 * part)),
        vm((2, 2, 2, down_rows, width)),
        vm((2, rows, wide)),
        vm((4, 3, rows, 2 * part)),
        vm((2, toks, width)),
        vm((2, toks, 128)),
        vm((4, toks, width)),
        vm((4, toks, width)),
        vm((2, toks, wide), F32),
        vm((2, toks + 8, half_width), F32),
        vm((2, toks, half_width), F32),
        vm((2, toks, half_width)),
        vm((2, toks, wide)),
        vm((toks, width), F32),
        vm((toks, width)),
        vm((toks, width)),
        vm((2, toks + 8, 2 * part), F32),
        vm((2 * toks, part), F32),
        vm((4, toks, 3 * part)),
        vm((3, 4, toks, 2 * part)),
        vm((4, toks, width), F32),
        vm((4, toks, width)),
        vm((half, width)),
        vm((half, width)),
        vm((toks, width)),
        vm((toks, width)),
        vm((2, toks, width)),
        vm((2, 2, 2, 4, rows, 2 * part)),
        vm((3, 2, 4, rows, 2 * part)),
        vm((3, 4, rows, 2 * part)),
        vm((2, 2, down_rows, width)),
        vm((2, down_rows, width)),
        vm((down_rows, width)),
        vm((2, 2, 2, 2, rows, wide)),
        vm((2, 2, 2, rows, wide)),
        vm((2, 2, rows, wide)),
        vm((2, rows, wide)),
        vm((2, 2, 2, rows, width)),
        vm((2, 2, rows, width)),
        vm((2, rows, width)),
        vm((rows, width)),
        vm((8, width + half_width), F32),
        pltpu.SemaphoreType.DMA((COPIES,)),
        pltpu.SemaphoreType.DMA((COPIES,)),
        pltpu.SemaphoreType.DMA((3,)),
        pltpu.SemaphoreType.DMA((20,)),
        pltpu.SemaphoreType.DMA((PLACES,)),
        pltpu.SemaphoreType.DMA((PLACES,)),
        pltpu.SemaphoreType.DMA((PLACES,)),
        pltpu.SemaphoreType.DMA((PLACES,)),
        pltpu.SemaphoreType.REGULAR,
        pltpu.SemaphoreType.REGULAR,
    ]
    outs = [
        jax.ShapeDtypeStruct((toks, width), BF16),
        jax.ShapeDtypeStruct((toks, width), F32),
        jax.ShapeDtypeStruct((8, 128), F32),
        jax.ShapeDtypeStruct((rows, 3 * width), F32),
        jax.ShapeDtypeStruct((rows, width), F32),
        jax.ShapeDtypeStruct((rows, ff), F32),
        jax.ShapeDtypeStruct((rows, ff), F32),
        jax.ShapeDtypeStruct((down_rows, width), F32),
    ]
    vmem = pl.BlockSpec(memory_space=pltpu.VMEM)
    hbm = pl.BlockSpec(memory_space=pl.ANY)
    result = pl.pallas_call(
        functools.partial(kernel, fsdp_count, spare, factor),
        out_shape=outs,
        in_specs=[vmem, hbm] + [vmem] * 6 + [hbm] + [vmem] * 2 + [hbm],
        out_specs=[hbm] + [vmem] * 2 + [hbm] * 5,
        scratch_shapes=scratch,
        compiler_params=pltpu.CompilerParams(
            collective_id=0, has_side_effects=True, vmem_limit_bytes=60 << 20
        ),
    )(
        tokens.reshape(toks, width),
        cotangent.reshape(toks, width),
        document_index,
        loss_token_mask,
        first_gain.reshape(1, rows),
        second_gain.reshape(1, rows),
        conv_kernel,
        mixer_in,
        mixer_out,
        gate_weight,
        up_weight,
        down_weight,
    )
    block_out, input_grad, small, g_mi, g_mo, g_gate, g_up, g_down = result
    number = lax.axis_index("dp") * fsdp_count + lax.axis_index("fsdp")
    place = number // spare
    own = lax.dynamic_slice_in_dim(small, (place % 4) * rows, rows, 1)

    def shared(item, axis=0):
        if spare == 1:
            return item
        return lax.psum_scatter(
            item, axes, scatter_dimension=axis, axis_index_groups=groups, tiled=True
        )

    return (
        block_out.reshape(row_count, seq_here, width),
        input_grad.reshape(row_count, seq_here, width),
        shared(own[0]),
        shared(g_mi),
        shared(own[2:5], 1),
        shared(g_mo),
        shared(own[1]),
        shared(g_gate),
        shared(g_up),
        shared(g_down),
    )


def solution(mesh):
    fsdp_count = mesh.shape["fsdp"]
    device_count = mesh.shape["dp"] * fsdp_count
    return jax.shard_map(
        functools.partial(per_device, fsdp_count, device_count),
        mesh=mesh,
        in_specs=(
            P("dp", "fsdp", None),
            P("dp", None),
            P("dp", "fsdp"),
            P("dp", "fsdp", None),
            P(("dp", "fsdp")),
            P(("dp", "fsdp"), None),
            P(None, ("dp", "fsdp")),
            P(("dp", "fsdp"), None),
            P(("dp", "fsdp")),
            P(("dp", "fsdp"), None),
            P(("dp", "fsdp"), None),
            P(("dp", "fsdp"), None),
        ),
        out_specs=(
            P("dp", "fsdp", None),
            P("dp", "fsdp", None),
            P(("dp", "fsdp")),
            P(("dp", "fsdp"), None),
            P(None, ("dp", "fsdp")),
            P(("dp", "fsdp"), None),
            P(("dp", "fsdp")),
            P(("dp", "fsdp"), None),
            P(("dp", "fsdp"), None),
            P(("dp", "fsdp"), None),
        ),
        check_vma=False,
    )
```

time: 1500 us -> 219 us (0.15)
  waiting for transfers between devices: 1230 us -> 0 us
  Pallas kernels: 0 us -> 208 us
  blocking collectives: 123 us -> 0 us
  matrix products: 93.6 us -> 0 us
  other arithmetic: 20.8 us -> 0 us
    reduce_scatter x5 -> x0, waiting for transfers between devices: 926 us -> none  [the longest x1 210 us: per_device(): lax.psum_scatter(local_grads[5], ('dp', 'fsdp'), scatter_dimension=0, til...]
    all_gather x5 -> x0, waiting for transfers between devices: 263 us -> none  [the longest x1 79.2 us: per_device(): lax.all_gather(shards[5], ('dp', 'fsdp'), axis=0, tiled=True)]
    pallas_call x0 -> x1, Pallas kernels: none -> 208 us  [per_device(): pl.pallas_call(functools.partial(kernel, fsdp_count, spare, factor), out_...]
    dot_general x15 -> x0, matrix products: 93.6 us -> none  [the longest x5 34.3 us: over_tokens(): lax.dot_general(left_side, right_side, (((0,), (0,)), ((), ())), preferre...]
    unnamed x2 -> x0, blocking collectives: 81.7 us -> none
    all_gather x1 -> x0, blocking collectives: 40.9 us -> none  [per_device(): lax.all_gather(shards[2], ('dp', 'fsdp'), axis=0, tiled=True)]
    unnamed x12 -> x0, waiting for transfers between devices: 37.9 us -> none
  transfers between devices with their start and end apart: 13 -> 0, of which waited for: 12 -> 0; matrix products, arithmetic and copies ran while one was open for 6% -> 0% of each run, Pallas kernels for 0% -> 0%
where the time goes in v1:
time: 219 us; the launch traced here: 218 us
  Pallas kernels  208 us (95%)
  local copies, waits for them, and re-layouts  10.1 us (5%)
    pallas_call x1, Pallas kernels, per_device(): pl.pallas_call(functools.partial(kernel, fsdp_count, spare, factor), out_...  208 us
    unnamed x19, local copies, waits for them, and re-layouts  8.12 us

profile of v1, /device:TPU:0, one launch (start us, length us, event | category | flops | bytes accessed | tf_op | source)
XLA Modules:
  0.0 218.3 jit_solution(4950637194925878869)
XLA Ops:
  0.7 207.5 %shard_map.195 = (bf16[256,1024]{1,0:T(8,128)(2,1)}, f32[256,1024]{1,0:T(8,128)}, f32[8,128]{1,0:T(8,128)}, f32[32,3072]{1,0:T(8,128)}, f32[32,1024]{1,0:T(8,128...) custom-call(bf16[256,1024]{1,0:T(8,128)(2,1)} %bitcast.12, bf16[256,1024]{1,0:T(8,128)(2,1)} %bitcast.13, ...), custom_call_target="tpu_custom_call" | custom-call | tf_op jit(solution)/shard_map/pallas_call | solution.py:1067
  208.2 0.0 copy-start
  208.2 0.8 constant_dynamic-slice_fusion
  209.0 0.6 slice.10
  209.6 0.5 slice_bitcast_fusion
  210.1 1.9 copy.29
  212.0 0.0 copy-done
  212.0 0.0 copy-start.4
  212.0 1.0 copy.30
  213.0 0.3 copy-done.4
  213.2 0.0 copy-start.5
  213.3 0.0 copy-start.3
  213.3 0.7 copy.31
  214.0 0.2 copy-done.5
  214.2 0.7 copy.32
  214.9 0.0 copy-done.3
  214.9 0.0 copy-start.2
  214.9 0.8 copy.33
  215.7 0.5 copy-done.2
  216.2 0.0 copy-start.1
  216.2 0.8 copy.34
  217.0 0.5 copy-done.1
  217.5 0.8 copy.35
Async XLA Ops:
  208.2 3.8 %copy-start = (f32[256,1024]{1,0:T(8,128)S(1)}, f32[256,1024]{1,0:T(8,128)}, u32[]{:S(2)}) copy-start(f32[256,1024]{1,0:T(8,128)} %get-tuple-element.19) | copy-start | bytes 3145732
  212.0 1.2 copy-start.4
  213.2 1.0 copy-start.5
  213.3 1.7 copy-start.3
  214.9 1.3 copy-start.2
  216.2 1.3 copy-start.1

commit v2 on v1

--- a/solution.py
+++ b/solution.py
@@ -46,11 +46,10 @@
     block_out,
     input_grad,
     small_out,
-    mixer_in_grad,
-    mixer_out_grad,
-    gate_grad,
-    up_grad,
-    down_grad,
+    mi_sum,
+    mo_sum,
+    gu_sum,
+    dn_sum,
     small_tile,
     small_all,
     small_grad,
@@ -215,8 +214,6 @@
 
     pl.semaphore_wait(barrier, PLACES + 1)
 
-    mi_swap = go(remote(mi_stage.at[1 - x], w_mi.at[z1, z0, y, x, c], xn))
-
     def small_copy(src, dst, m, sems=(small_send, small_recv)):
         return pltpu.make_async_remote_copy(
             src_ref=src, dst_ref=dst, send_sem=sems[0].at[m], recv_sem=sems[1].at[m],
@@ -227,6 +224,7 @@
         small_copy(small_tile, small_all.at[v], m).start()
         return 0
 
+    mi_swap = go(remote(mi_stage.at[1 - x], w_mi.at[z1, z0, y, x, c], xn))
     lax.fori_loop(1, PLACES, small_start, 0)
     tok_swap = go(remote(tokens, xs.at[x], xn))
 
@@ -235,6 +233,8 @@
 
     def mi_at(a, b, yy, cc):
         return w_mi.at[a, b, yy, :, cc]
+
+    every = slice(None)
 
     def mix_gather(at):
         return dict(
@@ -245,15 +245,17 @@
             y1=same(at(1 - z1, z0, y, c), yn),
             y2=same(at(z1, 1 - z0, y, c), yn),
             y3=same(at(1 - z1, 1 - z0, y, c), yn),
+            ca=same(at(every, every, y, c), cn),
+            cb=same(at(every, every, 1 - y, c), cn),
         )
 
     mo_g, mi_g = mix_gather(mo_at), mix_gather(mi_at)
+    mi_swap.wait_recv()
+    for name in ("s1", "s2", "y0"):
+        go(mi_g[name])
     load_out.wait()
     for name in ("s1", "s2", "y0"):
         go(mo_g[name])
-    mi_swap.wait_recv()
-    for name in ("s1", "s2", "y0"):
-        go(mi_g[name])
 
     offset = fs * toks
     ids = document[...].astype(F32) + 1.0
@@ -285,75 +287,83 @@
         gs[p, at, :] = (gs[p, at, :].astype(F32) * keep).astype(BF16)
         return 0
 
-    load_cot.wait()
-    lax.fori_loop(0, toks // step, flag_rows, 0)
-    flag_swap = go(same(flags.at[x], xn))
-    xs[x] = tokens[...]
-
     run = units // 4
+
     def pick(ref, at_p):
         whole = ref[...].astype(F32)
         return jnp.concatenate(
             [whole[:, run * (4 * z + at_p) : run * (4 * z + at_p) + run] for z in range(4)], axis=1
         ).astype(BF16)
 
+    def forward(g, arrived, names):
+        g[arrived].wait_recv()
+        for name in names:
+            go(g[name])
+
+    def z_gather(at):
+        return dict(
+            s1=same(at(z1, z0, c), z1n),
+            s2=same(at(z1, z0, c), z0n),
+            s3=same(at(1 - z1, z0, c), z0n),
+            core=same(at(every, every, c), cn),
+        )
+
+    dn_g = z_gather(lambda a, b, cc: w_dn.at[a, b, cc])
+    gu_g = [z_gather(lambda a, b, cc, j=j: w_gu.at[j, a, b, :, cc]) for j in range(3)]
+
+    def z_start(g):
+        go(g["s1"])
+        go(g["s2"])
+
+    def z_forward(g):
+        forward(g, "s1", ("s3",))
+
+    def z_core(g):
+        g["s2"].wait_recv()
+        g["s3"].wait_recv()
+        go(g["core"])
+
+    def plane_gather(buf, halves):
+        lo, hi = pl.ds(0, half), pl.ds(half, half)
+        return dict(
+            x0=same(buf.at[p, lo], xn),
+            y1=same(buf.at[p, hi], yn),
+            x1=same(buf.at[p, hi], xn),
+            y0=same(buf.at[p, lo], yn),
+            fx=same(buf.at[px, lo] if halves else buf.at[px], yn),
+            **(dict(fy=same(buf.at[py, hi], xn)) if halves else {}),
+        )
+
+    def plane_forward(g):
+        forward(g, "x0", ("fx",))
+        forward(g, "y1", ("fy",))
+
+    gs_g, hs_g = plane_gather(gs, False), plane_gather(hs, True)
+
+    load_cot.wait()
+    lax.fori_loop(0, toks // step, flag_rows, 0)
+    flag_swap = go(same(flags.at[x], xn))
     for at_p in range(4):
         picked_gate, picked_up = pick(gate, at_p), pick(up, at_p)
         for j in range(3):
             gu_stage[at_p, j, :, 0:part] = picked_gate[:, j * part : j * part + part]
             gu_stage[at_p, j, :, part:] = picked_up[:, j * part : j * part + part]
+    xs[x] = tokens[...]
     for j in range(3):
         w_gu[j, z1, z0, p, c] = gu_stage[p, j]
 
-    def forward(g, arrived, names):
-        g[arrived].wait_recv()
-        for name in names:
-            go(g[name])
-
-    for g in (mo_g, mi_g):
-        forward(g, "s1", ("s3", "y1"))
-        forward(g, "s2", ("y2",))
-        forward(g, "s3", ("y3",))
-
+    forward(mi_g, "s1", ("s3", "y1"))
+    forward(mi_g, "s2", ("y2",))
     gu_swap = [
         go(remote(gu_stage.at[px], w_gu.at[:, z1, z0, p, c], xn)),
         go(remote(gu_stage.at[py], w_gu.at[:, z1, z0, p, c], yn)),
         go(remote(gu_stage.at[pd], w_gu.at[:, z1, z0, p, c], dn)),
     ]
-
-    def z_gather(at):
-        return dict(
-            s1=same(at(z1, z0, c), z1n),
-            s2=same(at(z1, z0, c), z0n),
-            s3=same(at(1 - z1, z0, c), z0n),
-            core=same(at(slice(None), slice(None), c), cn),
-        )
-
-    dn_g = z_gather(lambda a, b, cc: w_dn.at[a, b, cc])
-    gu_g = [z_gather(lambda a, b, cc, j=j: w_gu.at[j, a, b, :, cc]) for j in range(3)]
+    go(gs_g["x0"])
+    go(gs_g["x1"])
+    forward(mo_g, "s1", ("s3",))
     load_down.wait()
-    go(dn_g["s1"])
-    go(dn_g["s2"])
-
-    def plane_gather(buf):
-        lo, hi = pl.ds(0, half), pl.ds(half, half)
-        g = dict(
-            x0=same(buf.at[p, lo], xn),
-            y1=same(buf.at[p, hi], yn),
-            x1=same(buf.at[p, hi], xn),
-            y0=same(buf.at[p, lo], yn),
-            fx=same(buf.at[px, lo], yn),
-            fy=same(buf.at[py, hi], xn),
-        )
-        for name in ("x0", "y1", "x1", "y0"):
-            go(g[name])
-        return g
-
-    def plane_forward(g):
-        forward(g, "x0", ("fx",))
-        forward(g, "y1", ("fy",))
-
-    gs_g = plane_gather(gs)
+    z_start(dn_g)
 
     def small_wait(m, _):
         copy = small_copy(small_tile, small_all.at[v], m)
@@ -398,17 +408,26 @@
 
         loop(toks, body)
 
+    forward(mi_g, "s3", ("y3",))
+    go(mi_g["ca"])
+    go(mo_g["y1"])
+    forward(mo_g, "s2", ("y2",))
+    forward(mo_g, "s3", ("y3",))
+    go(mo_g["ca"])
     hidden_one(x)
     tok_swap.wait_recv()
     hidden_one(1 - x)
-
-    for g in (mo_g, mi_g):
-        for name in ("y0", "y1", "y2", "y3"):
-            g[name].wait_recv()
-    every = slice(None)
-    mo_core = go(same(w_mo.at[:, :, :, c], cn))
-    mi_core = go(same(w_mi.at[:, :, :, :, c], cn))
-    mi_core.wait_recv()
+    z_forward(dn_g)
+    for copy in gu_swap:
+        copy.wait_recv()
+    z_start(gu_g[0])
+    for name in ("y0", "y1", "y2", "y3"):
+        mi_g[name].wait_recv()
+    go(mi_g["cb"])
+    go(gs_g["y1"])
+    go(gs_g["y0"])
+    mi_g["ca"].wait_recv()
+    mi_g["cb"].wait_recv()
     h1 = xs[...].reshape(2 * toks, width)
     wide = 3 * half_width
     proj[...] = nn(h1, w_mi[...].reshape(width, wide)).reshape(2, toks, wide)
@@ -421,6 +440,9 @@
 
         loop(toks, body)
     halo = go(remote(ubuf.at[:, pl.ds(toks, 8), :], ubuf.at[:, pl.ds(0, 8), :], following))
+    for name in ("y0", "y1", "y2", "y3"):
+        mo_g[name].wait_recv()
+    go(mo_g["cb"])
     flag_swap.wait_recv()
     halo.wait_recv()
     for s in range(2):
@@ -436,47 +458,35 @@
             ys[s, a : a + step, :] = (
                 proj[s, a : a + step, half_width : 2 * half_width] * value
             ).astype(BF16)
-    mo_core.wait_recv()
+    mo_g["ca"].wait_recv()
+    mo_g["cb"].wait_recv()
     mo_flat = w_mo[...].reshape(half_width, width)
     o_send[...] = nn(ys[1 - x], mo_flat).astype(BF16)
     o_swap = go(remote(o_send, o_recv, xn))
     x2[...] = nn(ys[x], mo_flat)
 
-    def z_forward(g):
-        forward(g, "s1", ("s3",))
-
-    def z_core(g):
-        g["s2"].wait_recv()
-        g["s3"].wait_recv()
-        go(g["core"])
-
-    z_forward(dn_g)
-    plane_forward(gs_g)
+    z_forward(gu_g[0])
+    z_start(gu_g[1])
+    forward(gs_g, "x0", ())
+    forward(gs_g, "x1", ("fx",))
+    z_core(dn_g)
     for copy in gu_swap:
-        copy.wait_recv()
         sent(copy)
     sent(mi_swap)
-    go(gu_g[0]["s1"])
-    go(gu_g[0]["s2"])
-    z_core(dn_g)
-
-    o_swap.wait_recv()
 
     def second_body(at):
         values = tokens[at, :].astype(F32) + x2[at, :] + o_recv[at, :].astype(F32)
         x2[at, :] = values
         hs[p, at, :] = (values * inverse_rms(values) * g2).astype(BF16)
 
+    o_swap.wait_recv()
     loop(toks, second_body)
-    hs_g = plane_gather(hs)
-    z_forward(gu_g[0])
-    go(gu_g[1]["s1"])
-    go(gu_g[1]["s2"])
+    for name in ("x0", "y1", "x1", "y0"):
+        go(hs_g[name])
+    z_start(gu_g[2])
+    z_core(gu_g[0])
     plane_forward(hs_g)
-    z_core(gu_g[0])
     z_forward(gu_g[1])
-    go(gu_g[2]["s1"])
-    go(gu_g[2]["s2"])
 
     ya, yb = 2 * y, 2 * (1 - y)
 
@@ -555,15 +565,6 @@
         add_rows(buf, py, 0, r_a)
         go(g["y0"])
 
-    dn_g["core"].wait_recv()
-    plane_pair(gs_g, ("x1",))
-    plane_pair(hs_g, ("x1",))
-    gu_g[0]["core"].wait_recv()
-    feed(0, ya)
-    plane_pair(gs_g, ("y0", "fx", "fy"))
-    plane_pair(hs_g, ("y0", "fx", "fy"))
-    feed(0, yb)
-
     def z_reduce(at, r_c, r_0, r_1):
         return dict(
             core=remote(at(every, every, 1 - c), r_c, cn),
@@ -593,34 +594,38 @@
             w_gu[j, a, z0, :, c] = plus(w_gu[j, a, z0, :, c], r_gu_0[j, a])
         go(gu_r[j]["z1"])
 
-    def gu_after_z1(j):
+    gu_back = []
+
+    def gu_sum_z1(j):
         gu_r[j]["z1"].wait_recv()
         w_gu[j, z1, z0, :, c] = plus(w_gu[j, z1, z0, :, c], r_gu_1[j])
         gu_stage[p, j] = w_gu[j, z1, z0, p, c]
-        return [
-            go(remote(w_gu.at[j, z1, z0, px, c], gu_stage.at[p, j], xn)),
-            go(remote(w_gu.at[j, z1, z0, py, c], gu_stage.at[p, j], yn)),
-            go(remote(w_gu.at[j, z1, z0, pd, c], gu_stage.at[p, j], dn)),
-        ]
+
+    def gu_return(j):
+        for place, target in ((px, xn), (py, yn), (pd, dn)):
+            gu_back.append(go(remote(w_gu.at[j, z1, z0, place, c], gu_stage.at[p, j], target)))
 
     def gathered(g):
         for name in ("s1", "s2", "s3", "core"):
             sent(g[name])
 
+    dn_g["core"].wait_recv()
+    plane_pair(hs_g, ("x1",))
+    gu_g[0]["core"].wait_recv()
+    feed(0, ya)
+    plane_pair(gs_g, ("y0", "y1", "fx"))
+    z_core(gu_g[1])
+    plane_pair(hs_g, ("y0", "fx", "fy"))
+    feed(0, yb)
+    z_forward(gu_g[2])
+    gu_g[1]["core"].wait_recv()
+    feed(1, yb)
     gathered(gu_g[0])
     gu_weight_grad(0)
     go(gu_r[0]["core"])
-    z_core(gu_g[1])
-    z_forward(gu_g[2])
+    feed(1, ya)
+    z_core(gu_g[2])
     gu_after_core(0)
-    gu_g[1]["core"].wait_recv()
-    feed(1, ya)
-    feed(1, yb)
-    gathered(gu_g[1])
-    gu_weight_grad(1)
-    go(gu_r[1]["core"])
-    z_core(gu_g[2])
-    gu_after_core(1)
     gu_g[2]["core"].wait_recv()
     feed(2, yb)
     dh_g = plane_scatter(dhp, dh_a, dh_b, dh_x, dh_y)
@@ -629,12 +634,15 @@
     go(dh_g["y1"])
     feed(2, ya)
     go(dh_g["x0"])
+    gathered(gu_g[1])
+    gu_weight_grad(1)
+    go(gu_r[1]["core"])
+    scatter_rest(dh_g, dhp, dh_a, dh_b)
+    gu_after_core(1)
+    gu_after_z0(0)
     gathered(gu_g[2])
     gu_weight_grad(2)
     go(gu_r[2]["core"])
-    scatter_rest(dh_g, dhp, dh_a, dh_b)
-    gu_after_z0(0)
-    gu_after_core(2)
 
     for name in ("x0", "x1", "y0", "y1", "fx", "fy"):
         sent(hs_g[name])
@@ -649,7 +657,7 @@
         .reshape(w_dn.shape)
     )
     go(dn_r["core"])
-    gu_after_z0(1)
+    gu_after_core(2)
 
     for name in ("x0", "x1", "y0", "y1"):
         dh_g[name].wait_recv()
@@ -670,16 +678,17 @@
 
     loop(toks, norm_two)
     do_swap = go(same(dos.at[x], xn))
-    lo, hi = pl.ds(0, half), pl.ds(half, half)
-    ou_g = plane_scatter(hs, dhp.at[py, lo], dhp.at[px, hi], dhp.at[p], dhp.at[p])
+    ou_b = remote(hs.at[pd], dhp.at[px], yn)
+    ou_y = remote(hs.at[py], dhp.at[p], yn)
+    ou_x = remote(hs.at[px], dhp.at[p], xn)
     for copy in dh_g.values():
         sent(copy)
     pl.semaphore_signal(free_x, inc=1, device_id=xn, device_id_type=MESH)
     pl.semaphore_signal(free_y, inc=1, device_id=yn, device_id_type=MESH)
     pl.semaphore_wait(free_x, 1)
     pl.semaphore_wait(free_y, 1)
-    for name in ("a", "b", "x0", "y1"):
-        go(ou_g[name])
+    go(ou_b)
+    go(ou_y)
 
     mo_flat = w_mo[...].reshape(half_width, width)
 
@@ -693,11 +702,13 @@
 
     dkbuf[x, 0:toks, 0:half_width] = nt(dos[x], mo_flat)
     split_dy(x)
+    gu_after_z0(1)
     dn_r["core"].wait_recv()
     for a in range(2):
         for b in range(2):
             w_dn[a, b, c] = plus(w_dn[a, b, c], r_dn_c[a, b])
     go(dn_r["z0"])
+    gu_sum_z1(0)
     do_swap.wait_recv()
     dkbuf[1 - x, 0:toks, 0:half_width] = nt(dos[1 - x], mo_flat)
     split_dy(1 - x)
@@ -708,11 +719,9 @@
             preceding,
         )
     )
-    for name in ("s1", "s2", "s3", "y0", "y1", "y2", "y3"):
-        sent(mo_g[name])
-        sent(mi_g[name])
-    sent(mo_core)
-    sent(mi_core)
+    for g in (mo_g, mi_g):
+        for copy in g.values():
+            sent(copy)
     w_mo[...] = (
         tn(ys[...].reshape(2 * toks, half_width), dos[...].reshape(2 * toks, width))
         .astype(BF16)
@@ -734,6 +743,20 @@
     mo_r = mix_reduce(mo_at, r_mo_c, r_mo_y, r_mo_0, r_mo_1)
     mi_r = mix_reduce(mi_at, r_mi_c, r_mi_y, r_mi_0, r_mi_1)
     go(mo_r["core"])
+    gu_after_z0(2)
+
+    def mix_core(w, r_c, g, with_x):
+        g["core"].wait_recv()
+        for a in range(2):
+            for b in range(2):
+                for yy in range(2):
+                    if with_x:
+                        w[a, b, yy, :, c] = plus(w[a, b, yy, :, c], r_c[a, b, yy])
+                    else:
+                        w[a, b, yy, c] = plus(w[a, b, yy, c], r_c[a, b, yy])
+        for name in ("y3", "y1", "y2", "y0"):
+            go(g[name])
+
     dk_halo.wait_recv()
     ek = [jnp.zeros((1, half_width), F32) for _ in range(3)]
     for s in range(2):
@@ -768,6 +791,7 @@
             small_grad[2 + k : 3 + k, 256 * q : 256 * q + 128] = even[0:1]
             small_grad[2 + k : 3 + k, 256 * q + 128 : 256 * q + 256] = odd[0:1]
 
+    mix_core(w_mo, r_mo_c, mo_r, False)
     mi_flat = w_mi[...].reshape(width, wide)
     sent(o_swap)
     o_send[...] = nt(dps[1 - x], mi_flat).astype(BF16)
@@ -779,23 +803,18 @@
         .reshape(w_mi.shape)
     )
     go(mi_r["core"])
-    scatter_rest(ou_g, hs, dhp.at[pd, lo], dhp.at[pd, hi])
-    gu_after_z0(2)
-
-    def mix_core(w, r_c, g, with_x):
-        g["core"].wait_recv()
-        for a in range(2):
-            for b in range(2):
-                for yy in range(2):
-                    if with_x:
-                        w[a, b, yy, :, c] = plus(w[a, b, yy, :, c], r_c[a, b, yy])
-                    else:
-                        w[a, b, yy, c] = plus(w[a, b, yy, c], r_c[a, b, yy])
-        for name in ("y3", "y2", "y1", "y0"):
-            go(g[name])
-
-    mix_core(w_mo, r_mo_c, mo_r, False)
+
     mix_core(w_mi, r_mi_c, mi_r, True)
+    ou_b.wait_recv()
+
+    def far_part(at):
+        hs[px, at, :] = (hs[px, at, :].astype(F32) + dhp[pd, at, :].astype(F32)).astype(BF16)
+
+    loop(toks, far_part)
+    gu_sum_z1(1)
+    gu_return(0)
+    gu_return(1)
+    go(ou_x)
 
     dn_r["z0"].wait_recv()
     for a in range(2):
@@ -832,9 +851,6 @@
     lax.fori_loop(1, PLACES, small_back_start, 0)
     small_in[v] = small_in[PLACES + lax.div(v, 4)]
 
-    gu_back = gu_after_z1(0)
-    gu_back += gu_after_z1(1)
-
     def mo_idx(a, b):
         return (a, b, y, c)
 
@@ -848,25 +864,25 @@
         g["y3"].wait_recv()
         add(1 - z1, 1 - z0, r_y[1 - z1, 1 - z0])
         go(g["s3"])
-        g["y2"].wait_recv()
-        add(z1, 1 - z0, r_y[z1, 1 - z0])
-        go(g["s2"])
         g["y1"].wait_recv()
         add(1 - z1, z0, r_y[1 - z1, z0])
         g["s3"].wait_recv()
         add(1 - z1, z0, r_0[1 - z1])
         go(g["s1"])
+        g["y2"].wait_recv()
+        add(z1, 1 - z0, r_y[z1, 1 - z0])
+        go(g["s2"])
         g["y0"].wait_recv()
         add(z1, z0, r_y[z1, z0])
         g["s2"].wait_recv()
         add(z1, z0, r_0[z1])
 
     mix_rest(w_mo, mo_idx, mo_r, r_mo_y, r_mo_0, r_mo_1)
+    gu_sum_z1(2)
+    gu_return(2)
     mix_rest(w_mi, mi_idx, mi_r, r_mi_y, r_mi_0, r_mi_1)
-    gu_back += gu_after_z1(2)
-
-    for name in ("x0", "x1", "y0", "y1"):
-        ou_g[name].wait_recv()
+    ou_x.wait_recv()
+    ou_y.wait_recv()
 
     def out_body(at):
         o_send[at, :] = (
@@ -890,10 +906,10 @@
     down_rows = w_dn.shape[3]
     dn_r["z1"].wait_recv()
     acc[3, 0:down_rows] = (w_dn[z1, z0, c].astype(F32) + r_dn_1[...].astype(F32)) * factor
-    store(acc.at[3, pl.ds(0, down_rows)], down_grad)
+    store(acc.at[3, pl.ds(0, down_rows)], dn_sum)
     mo_r["s1"].wait_recv()
     acc[2, 96 : 96 + rows] = (w_mo[z1, z0, y, c].astype(F32) + r_mo_1[...].astype(F32)) * factor
-    store(acc.at[2, pl.ds(96, rows)], mixer_out_grad)
+    store(acc.at[2, pl.ds(96, rows)], mo_sum)
     mi_r["s1"].wait_recv()
     w_mi[z1, z0, y, :, c] = plus(w_mi[z1, z0, y, :, c], r_mi_1[...])
     mi_stage[x] = w_mi[z1, z0, y, x, c]
@@ -901,33 +917,9 @@
 
     for copy in gu_back:
         copy.wait_recv()
-    for slot, (ref, start) in enumerate(((gate_grad, 0), (up_grad, part))):
-        pieces = []
-        for at_p in range(4):
-            whole = jnp.concatenate(
-                [gu_stage[at_p, j, :, start : start + part] for j in range(3)], axis=1
-            ).astype(F32)
-            pieces.append(whole * factor)
-        whole = jnp.concatenate(
-            [pieces[q % 4][:, run * (q // 4) : run * (q // 4) + run] for q in range(16)], axis=1
-        )
-        for k, first in enumerate(range(0, whole.shape[1], width)):
-            count = min(width, whole.shape[1] - first)
-            acc[slot, k * rows : k * rows + rows, 0:count] = whole[:, first : first + count]
-            store(
-                acc.at[slot, pl.ds(k * rows, rows), pl.ds(0, count)],
-                ref.at[:, pl.ds(first, count)],
-            )
+    store(gu_stage, gu_sum)
     mi_back.wait_recv()
-    for b in range(3):
-        for q in range(width // 256):
-            at = b * half_width + 128 * q
-            first = mi_stage[0, :, at : at + 128].astype(F32) * factor
-            second = mi_stage[1, :, at : at + 128].astype(F32) * factor
-            to, block = 256 * q, pl.ds(b * rows, rows)
-            acc[2, block, to : to + 128] = jnp.where(low, first, pltpu.roll(second, 64, 1))
-            acc[2, block, to + 128 : to + 256] = jnp.where(low, pltpu.roll(first, 64, 1), second)
-        store(acc.at[2, pl.ds(b * rows, rows)], mixer_in_grad.at[:, pl.ds(b * width, width)])
+    store(mi_stage, mi_sum)
 
     def small_back_wait(m, _):
         small_back(m).wait()
@@ -947,6 +939,66 @@
 
 
 COPIES = 160
+
+
+def finish(
+    fsdp_count,
+    copies_of_place,
+    factor,
+    block_sum,
+    input_sum,
+    small,
+    mi_sum,
+    mo_sum,
+    gu_sum,
+    dn_sum,
+    block_out,
+    input_grad,
+    gain_one_grad,
+    mixer_in_grad,
+    taps_grad,
+    mixer_out_grad,
+    gain_two_grad,
+    gate_grad,
+    up_grad,
+    down_grad,
+):
+    input_grad[...] = input_sum[...]
+    block_out[...] = block_sum[...]
+    down_grad[...] = dn_sum[...]
+    mixer_out_grad[...] = mo_sum[...]
+    rows, ff = gate_grad.shape
+    width = mixer_out_grad.shape[1]
+    part, run, half_width = ff // 12, ff // 16, width // 2
+    for ref, start in ((gate_grad, 0), (up_grad, part)):
+        pieces = [
+            jnp.concatenate(
+                [gu_sum[at_p, j, :, start : start + part] for j in range(3)], axis=1
+            ).astype(F32)
+            * factor
+            for at_p in range(4)
+        ]
+        ref[...] = jnp.concatenate(
+            [pieces[q % 4][:, run * (q // 4) : run * (q // 4) + run] for q in range(16)], axis=1
+        )
+    low = lax.broadcasted_iota(jnp.int32, (rows, 128), 1) < 64
+    for b in range(3):
+        for q in range(width // 256):
+            at = b * half_width + 128 * q
+            first = mi_sum[0, :, at : at + 128].astype(F32) * factor
+            second = mi_sum[1, :, at : at + 128].astype(F32) * factor
+            to = b * width + 256 * q
+            mixer_in_grad[:, to : to + 128] = jnp.where(low, first, pltpu.roll(second, 64, 1))
+            mixer_in_grad[:, to + 128 : to + 256] = jnp.where(low, pltpu.roll(first, 64, 1), second)
+    number = lax.axis_index("dp") * fsdp_count + lax.axis_index("fsdp")
+    quarter = lax.rem(lax.div(number, copies_of_place), 4)
+    values = small[...]
+    own = values[:, 0:rows]
+    for k in range(1, 4):
+        own = jnp.where(quarter == k, values[:, k * rows : k * rows + rows], own)
+    gain_one_grad[...] = own[0:1]
+    gain_two_grad[...] = own[1:2]
+    taps_grad[...] = own[2:5]
 
 
 def per_device(
@@ -1056,10 +1108,9 @@
         jax.ShapeDtypeStruct((toks, width), BF16),
         jax.ShapeDtypeStruct((toks, width), F32),
         jax.ShapeDtypeStruct((8, 128), F32),
-        jax.ShapeDtypeStruct((rows, 3 * width), F32),
+        jax.ShapeDtypeStruct((2, rows, wide), BF16),
         jax.ShapeDtypeStruct((rows, width), F32),
-        jax.ShapeDtypeStruct((rows, ff), F32),
-        jax.ShapeDtypeStruct((rows, ff), F32),
+        jax.ShapeDtypeStruct((4, 3, rows, 2 * part), BF16),
         jax.ShapeDtypeStruct((down_rows, width), F32),
     ]
     vmem = pl.BlockSpec(memory_space=pltpu.VMEM)
@@ -1068,7 +1119,7 @@
         functools.partial(kernel, fsdp_count, spare, factor),
         out_shape=outs,
         in_specs=[vmem, hbm] + [vmem] * 6 + [hbm] + [vmem] * 2 + [hbm],
-        out_specs=[hbm] + [vmem] * 2 + [hbm] * 5,
+        out_specs=[hbm] + [vmem] * 2 + [hbm] * 4,
         scratch_shapes=scratch,
         compiler_params=pltpu.CompilerParams(
             collective_id=0, has_side_effects=True, vmem_limit_bytes=60 << 20
@@ -1087,10 +1138,25 @@
         up_weight,
         down_weight,
     )
-    block_out, input_grad, small, g_mi, g_mo, g_gate, g_up, g_down = result
-    number = lax.axis_index("dp") * fsdp_count + lax.axis_index("fsdp")
-    place = number // spare
-    own = lax.dynamic_slice_in_dim(small, (place % 4) * rows, rows, 1)
+    finished = pl.pallas_call(
+        functools.partial(finish, fsdp_count, spare, factor),
+        out_shape=[
+            jax.ShapeDtypeStruct((toks, width), BF16),
+            jax.ShapeDtypeStruct((toks, width), F32),
+            jax.ShapeDtypeStruct((1, rows), F32),
+            jax.ShapeDtypeStruct((rows, 3 * width), F32),
+            jax.ShapeDtypeStruct((3, rows), F32),
+            jax.ShapeDtypeStruct((rows, width), F32),
+            jax.ShapeDtypeStruct((1, rows), F32),
+            jax.ShapeDtypeStruct((rows, ff), F32),
+            jax.ShapeDtypeStruct((rows, ff), F32),
+            jax.ShapeDtypeStruct((down_rows, width), F32),
+        ],
+        in_specs=[vmem] * 7,
+        out_specs=[vmem] * 10,
+        compiler_params=pltpu.CompilerParams(vmem_limit_bytes=60 << 20),
+    )(*result)
+    block_out, input_grad, g_one, g_mi, g_taps, g_mo, g_two, g_gate, g_up, g_down = finished
 
     def shared(item, axis=0):
         if spare == 1:
@@ -1102,11 +1168,11 @@
     return (
         block_out.reshape(row_count, seq_here, width),
         input_grad.reshape(row_count, seq_here, width),
-        shared(own[0]),
+        shared(g_one.reshape(rows)),
         shared(g_mi),
-        shared(own[2:5], 1),
+        shared(g_taps, 1),
         shared(g_mo),
-        shared(own[1]),
+        shared(g_two.reshape(rows)),
         shared(g_gate),
         shared(g_up),
         shared(g_down),

time: 219 us -> 207 us (0.945)
  local copies, waits for them, and re-layouts: 10.1 us -> 0 us
    unnamed x19 -> x0, local copies, waits for them, and re-layouts: 8.12 us -> none
    pallas_call x1, Pallas kernels: 208 us -> 202 us  [per_device(): pl.pallas_call(functools.partial(kernel, fsdp_count, spare, factor), out_...]
    pallas_call x0 -> x1, Pallas kernels: none -> 4.23 us  [per_device(): pl.pallas_call(functools.partial(finish, fsdp_count, spare, factor), out_...]
where the time goes in v2:
time: 207 us
  Pallas kernels  206 us (100%)
    pallas_call x1, Pallas kernels, per_device(): pl.pallas_call(functools.partial(kernel, fsdp_count, spare, factor), out_...  202 us
    pallas_call x1, Pallas kernels, per_device(): pl.pallas_call(functools.partial(finish, fsdp_count, spare, factor), out_...  4.23 us

profile of v2, /device:TPU:0, one launch (start us, length us, event | category | flops | bytes accessed | tf_op | source)
XLA Modules:
  0.0 206.6 jit_solution(10129338384454974798)
XLA Ops:
  0.6 201.7 %shard_map.195 = (bf16[256,1024]{1,0:T(8,128)(2,1)}, f32[256,1024]{1,0:T(8,128)}, f32[8,128]{1,0:T(8,128)}, bf16[2,32,1536]{2,1,0:T(8,128)(2,1)}, f32[32,1024]{1...) custom-call(bf16[256,1024]{1,0:T(8,128)(2,1)} %bitcast.8, bf16[256,1024]{1,0:T(8,128)(2,1)} %bitcast.9, ...), custom_call_target="tpu_custom_call" | custom-call | tf_op jit(solution)/shard_map/pallas_call | solution.py:1118
  202.4 4.2 %shard_map.196 = (bf16[256,1024]{1,0:T(8,128)(2,1)}, f32[256,1024]{1,0:T(8,128)}, f32[1,32]{1,0:T(1,128)}, f32[32,3072]{1,0:T(8,128)}, f32[3,32]{1,0:T(4,128)}, ...) custom-call(bf16[256,1024]{1,0:T(8,128)(2,1)} %get-tuple-element.27., ...), custom_call_target="tpu_custom_call" | custom-call | tf_op jit(solution)/shard_map/pallas_call | solution.py:1141

commit v3 on v2

--- a/solution.py
+++ b/solution.py
@@ -31,25 +31,30 @@
     fsdp_count,
     copies_of_place,
     factor,
-    tokens,
+    tokens_hbm,
     cotangent,
     document,
     loss_mask,
     gain_one,
     gain_two,
     taps,
-    mixer_in,
+    mixer_in_hbm,
     mixer_out,
-    gate,
-    up,
+    gate_hbm,
+    up_hbm,
     down,
     block_out,
-    input_grad,
+    input_sum,
     small_out,
     mi_sum,
     mo_sum,
     gu_sum,
     dn_sum,
+    input_grad,
+    tokens,
+    mixer_in,
+    gate,
+    up,
     small_tile,
     small_all,
     small_grad,
@@ -180,12 +185,20 @@
     pl.semaphore_signal(barrier, inc=1, device_id=following, device_id_type=MESH)
     pl.semaphore_signal(barrier, inc=1, device_id=preceding, device_id_type=MESH)
 
+    load_mixer = pltpu.make_async_copy(mixer_in_hbm, mixer_in, load_sem.at[3])
+    load_tokens = pltpu.make_async_copy(tokens_hbm, tokens, load_sem.at[4])
+    load_gate = pltpu.make_async_copy(gate_hbm, gate, load_sem.at[5])
+    load_up = pltpu.make_async_copy(up_hbm, up, load_sem.at[6])
+    load_mixer.start()
     load_out = pltpu.make_async_copy(mixer_out, w_mo.at[z1, z0, y, c], load_sem.at[0])
     load_down = pltpu.make_async_copy(down, w_dn.at[z1, z0, c], load_sem.at[1])
     load_cot = pltpu.make_async_copy(cotangent, gs.at[p], load_sem.at[2])
     load_out.start()
     load_down.start()
     load_cot.start()
+    load_gate.start()
+    load_up.start()
+    load_tokens.start()
 
     lane = lax.broadcasted_iota(jnp.int32, (1, 128), 1)
     mine = lax.div(lane, 32) == lax.rem(v, 4)
@@ -201,6 +214,7 @@
 
     lanes128 = lax.broadcasted_iota(jnp.int32, (rows, 128), 1)
     low = lanes128 < 64
+    load_mixer.wait()
     for b in range(3):
         for q in range(width // 256):
             at = b * width + 256 * q
@@ -226,7 +240,7 @@
 
     mi_swap = go(remote(mi_stage.at[1 - x], w_mi.at[z1, z0, y, x, c], xn))
     lax.fori_loop(1, PLACES, small_start, 0)
-    tok_swap = go(remote(tokens, xs.at[x], xn))
+    tok_swap = go(remote(tokens_hbm, xs.at[x], xn))
 
     def mo_at(a, b, yy, cc):
         return w_mo.at[a, b, yy, cc]
@@ -249,13 +263,18 @@
             cb=same(at(every, every, 1 - y, c), cn),
         )
 
-    mo_g, mi_g = mix_gather(mo_at), mix_gather(mi_at)
+    wide = 3 * half_width
+
+    def mi_half(h):
+        columns = pl.ds(h * (wide // 2), wide // 2)
+        return lambda a, b, yy, cc: w_mi.at[a, b, yy, :, cc, :, columns]
+
+    mo_g = mix_gather(mo_at)
+    mi_gs = [mix_gather(mi_half(0)), mix_gather(mi_half(1))]
     mi_swap.wait_recv()
-    for name in ("s1", "s2", "y0"):
-        go(mi_g[name])
-    load_out.wait()
-    for name in ("s1", "s2", "y0"):
-        go(mo_g[name])
+    for g in mi_gs:
+        for name in ("s1", "s2", "y0"):
+            go(g[name])
 
     offset = fs * toks
     ids = document[...].astype(F32) + 1.0
@@ -343,27 +362,33 @@
     load_cot.wait()
     lax.fori_loop(0, toks // step, flag_rows, 0)
     flag_swap = go(same(flags.at[x], xn))
+    load_gate.wait()
+    load_up.wait()
     for at_p in range(4):
         picked_gate, picked_up = pick(gate, at_p), pick(up, at_p)
         for j in range(3):
             gu_stage[at_p, j, :, 0:part] = picked_gate[:, j * part : j * part + part]
             gu_stage[at_p, j, :, part:] = picked_up[:, j * part : j * part + part]
+    load_tokens.wait()
     xs[x] = tokens[...]
     for j in range(3):
         w_gu[j, z1, z0, p, c] = gu_stage[p, j]
 
-    forward(mi_g, "s1", ("s3", "y1"))
-    forward(mi_g, "s2", ("y2",))
+    for g in mi_gs:
+        forward(g, "s1", ("s3", "y1"))
+        forward(g, "s2", ("y2",))
+    load_out.wait()
+    go(mo_g["s1"])
+    go(mo_g["s2"])
     gu_swap = [
-        go(remote(gu_stage.at[px], w_gu.at[:, z1, z0, p, c], xn)),
-        go(remote(gu_stage.at[py], w_gu.at[:, z1, z0, p, c], yn)),
-        go(remote(gu_stage.at[pd], w_gu.at[:, z1, z0, p, c], dn)),
+        remote(gu_stage.at[px], w_gu.at[:, z1, z0, p, c], xn),
+        remote(gu_stage.at[py], w_gu.at[:, z1, z0, p, c], yn),
+        remote(gu_stage.at[pd], w_gu.at[:, z1, z0, p, c], dn),
     ]
+    go(gu_swap[2])
+    go(gu_swap[0])
     go(gs_g["x0"])
     go(gs_g["x1"])
-    forward(mo_g, "s1", ("s3",))
-    load_down.wait()
-    z_start(dn_g)
 
     def small_wait(m, _):
         copy = small_copy(small_tile, small_all.at[v], m)
@@ -408,28 +433,30 @@
 
         loop(toks, body)
 
-    forward(mi_g, "s3", ("y3",))
-    go(mi_g["ca"])
-    go(mo_g["y1"])
+    for g in mi_gs:
+        forward(g, "s3", ("y3",))
+        go(g["ca"])
+    go(gu_swap[1])
+    go(mo_g["y0"])
+    forward(mo_g, "s1", ("s3", "y1"))
+    load_down.wait()
+    z_start(dn_g)
+    hidden_one(x)
+    tok_swap.wait_recv()
+    hidden_one(1 - x)
     forward(mo_g, "s2", ("y2",))
     forward(mo_g, "s3", ("y3",))
     go(mo_g["ca"])
-    hidden_one(x)
-    tok_swap.wait_recv()
-    hidden_one(1 - x)
-    z_forward(dn_g)
-    for copy in gu_swap:
-        copy.wait_recv()
-    z_start(gu_g[0])
-    for name in ("y0", "y1", "y2", "y3"):
-        mi_g[name].wait_recv()
-    go(mi_g["cb"])
+    for g in mi_gs:
+        for name in ("y0", "y1", "y2", "y3"):
+            g[name].wait_recv()
+        go(g["cb"])
     go(gs_g["y1"])
     go(gs_g["y0"])
-    mi_g["ca"].wait_recv()
-    mi_g["cb"].wait_recv()
+    for g in mi_gs:
+        g["ca"].wait_recv()
+        g["cb"].wait_recv()
     h1 = xs[...].reshape(2 * toks, width)
-    wide = 3 * half_width
     proj[...] = nn(h1, w_mi[...].reshape(width, wide)).reshape(2, toks, wide)
 
     for s in range(2):
@@ -440,6 +467,11 @@
 
         loop(toks, body)
     halo = go(remote(ubuf.at[:, pl.ds(toks, 8), :], ubuf.at[:, pl.ds(0, 8), :], following))
+    z_forward(dn_g)
+    for copy in gu_swap:
+        copy.wait_recv()
+    z_start(gu_g[0])
+    z_start(gu_g[1])
     for name in ("y0", "y1", "y2", "y3"):
         mo_g[name].wait_recv()
     go(mo_g["cb"])
@@ -465,8 +497,6 @@
     o_swap = go(remote(o_send, o_recv, xn))
     x2[...] = nn(ys[x], mo_flat)
 
-    z_forward(gu_g[0])
-    z_start(gu_g[1])
     forward(gs_g, "x0", ())
     forward(gs_g, "x1", ("fx",))
     z_core(dn_g)
@@ -483,10 +513,11 @@
     loop(toks, second_body)
     for name in ("x0", "y1", "x1", "y0"):
         go(hs_g[name])
+    z_forward(gu_g[0])
+    z_forward(gu_g[1])
     z_start(gu_g[2])
+    plane_forward(hs_g)
     z_core(gu_g[0])
-    plane_forward(hs_g)
-    z_forward(gu_g[1])
 
     ya, yb = 2 * y, 2 * (1 - y)
 
@@ -613,19 +644,19 @@
     plane_pair(hs_g, ("x1",))
     gu_g[0]["core"].wait_recv()
     feed(0, ya)
+    z_core(gu_g[1])
+    z_forward(gu_g[2])
     plane_pair(gs_g, ("y0", "y1", "fx"))
-    z_core(gu_g[1])
     plane_pair(hs_g, ("y0", "fx", "fy"))
     feed(0, yb)
-    z_forward(gu_g[2])
-    gu_g[1]["core"].wait_recv()
-    feed(1, yb)
     gathered(gu_g[0])
     gu_weight_grad(0)
     go(gu_r[0]["core"])
+    z_core(gu_g[2])
+    gu_g[1]["core"].wait_recv()
+    feed(1, yb)
+    gu_after_core(0)
     feed(1, ya)
-    z_core(gu_g[2])
-    gu_after_core(0)
     gu_g[2]["core"].wait_recv()
     feed(2, yb)
     dh_g = plane_scatter(dhp, dh_a, dh_b, dh_x, dh_y)
@@ -634,15 +665,15 @@
     go(dh_g["y1"])
     feed(2, ya)
     go(dh_g["x0"])
+    gu_after_z0(0)
     gathered(gu_g[1])
     gu_weight_grad(1)
     go(gu_r[1]["core"])
-    scatter_rest(dh_g, dhp, dh_a, dh_b)
-    gu_after_core(1)
-    gu_after_z0(0)
     gathered(gu_g[2])
     gu_weight_grad(2)
+    gu_after_core(1)
     go(gu_r[2]["core"])
+    scatter_rest(dh_g, dhp, dh_a, dh_b)
 
     for name in ("x0", "x1", "y0", "y1", "fx", "fy"):
         sent(hs_g[name])
@@ -650,6 +681,7 @@
     for base in (ya, yb):
         m = ms[pl.ds(base, 2)].reshape(2 * toks, units)
         hs[pl.ds(base, 2)] = nn(m, dn_flat).astype(BF16).reshape(2, toks, width)
+    gu_after_core(2)
     gathered(dn_g)
     w_dn[...] = (
         tn(ms[...].reshape(4 * toks, units), gs[...].reshape(4 * toks, width))
@@ -657,7 +689,11 @@
         .reshape(w_dn.shape)
     )
     go(dn_r["core"])
-    gu_after_core(2)
+    dn_r["core"].wait_recv()
+    for a in range(2):
+        for b in range(2):
+            w_dn[a, b, c] = plus(w_dn[a, b, c], r_dn_c[a, b])
+    go(dn_r["z0"])
 
     for name in ("x0", "x1", "y0", "y1"):
         dh_g[name].wait_recv()
@@ -678,17 +714,16 @@
 
     loop(toks, norm_two)
     do_swap = go(same(dos.at[x], xn))
-    ou_b = remote(hs.at[pd], dhp.at[px], yn)
-    ou_y = remote(hs.at[py], dhp.at[p], yn)
-    ou_x = remote(hs.at[px], dhp.at[p], xn)
+    lo, hi = pl.ds(0, half), pl.ds(half, half)
+    ou_g = plane_scatter(hs, dhp.at[py, lo], dhp.at[px, hi], dhp.at[p], dhp.at[p])
     for copy in dh_g.values():
         sent(copy)
     pl.semaphore_signal(free_x, inc=1, device_id=xn, device_id_type=MESH)
     pl.semaphore_signal(free_y, inc=1, device_id=yn, device_id_type=MESH)
     pl.semaphore_wait(free_x, 1)
     pl.semaphore_wait(free_y, 1)
-    go(ou_b)
-    go(ou_y)
+    for name in ("b", "y1", "a"):
+        go(ou_g[name])
 
     mo_flat = w_mo[...].reshape(half_width, width)
 
@@ -703,12 +738,8 @@
     dkbuf[x, 0:toks, 0:half_width] = nt(dos[x], mo_flat)
     split_dy(x)
     gu_after_z0(1)
-    dn_r["core"].wait_recv()
-    for a in range(2):
-        for b in range(2):
-            w_dn[a, b, c] = plus(w_dn[a, b, c], r_dn_c[a, b])
-    go(dn_r["z0"])
     gu_sum_z1(0)
+    gu_return(0)
     do_swap.wait_recv()
     dkbuf[1 - x, 0:toks, 0:half_width] = nt(dos[1 - x], mo_flat)
     split_dy(1 - x)
@@ -719,7 +750,7 @@
             preceding,
         )
     )
-    for g in (mo_g, mi_g):
+    for g in (mo_g, *mi_gs):
         for copy in g.values():
             sent(copy)
     w_mo[...] = (
@@ -730,7 +761,8 @@
 
     def mix_reduce(at, r_c, r_y, r_0, r_1):
         return dict(
-            core=remote(at(every, every, every, 1 - c), r_c, cn),
+            ca=remote(at(every, every, 1 - y, 1 - c), r_c.at[:, :, 1 - y], cn),
+            cb=remote(at(every, every, y, 1 - c), r_c.at[:, :, y], cn),
             y3=remote(at(1 - z1, 1 - z0, 1 - y, c), r_y.at[1 - z1, 1 - z0], yn),
             y2=remote(at(z1, 1 - z0, 1 - y, c), r_y.at[z1, 1 - z0], yn),
             y1=remote(at(1 - z1, z0, 1 - y, c), r_y.at[1 - z1, z0], yn),
@@ -742,20 +774,25 @@
 
     mo_r = mix_reduce(mo_at, r_mo_c, r_mo_y, r_mo_0, r_mo_1)
     mi_r = mix_reduce(mi_at, r_mi_c, r_mi_y, r_mi_0, r_mi_1)
-    go(mo_r["core"])
+    go(mo_r["ca"])
+    go(mo_r["cb"])
     gu_after_z0(2)
 
     def mix_core(w, r_c, g, with_x):
-        g["core"].wait_recv()
-        for a in range(2):
-            for b in range(2):
-                for yy in range(2):
+        def add(yy):
+            for a in range(2):
+                for b in range(2):
                     if with_x:
                         w[a, b, yy, :, c] = plus(w[a, b, yy, :, c], r_c[a, b, yy])
                     else:
                         w[a, b, yy, c] = plus(w[a, b, yy, c], r_c[a, b, yy])
+
+        g["ca"].wait_recv()
+        add(1 - y)
         for name in ("y3", "y1", "y2", "y0"):
             go(g[name])
+        g["cb"].wait_recv()
+        add(y)
 
     dk_halo.wait_recv()
     ek = [jnp.zeros((1, half_width), F32) for _ in range(3)]
@@ -791,36 +828,87 @@
             small_grad[2 + k : 3 + k, 256 * q : 256 * q + 128] = even[0:1]
             small_grad[2 + k : 3 + k, 256 * q + 128 : 256 * q + 256] = odd[0:1]
 
+    for q in range(8):
+        small_in[PLACES + q] = small_grad[:, 128 * q : 128 * q + 128]
+
+    def small_back(m):
+        target = lax.rem(v + m, PLACES)
+        source = small_in.at[PLACES + lax.div(target, 4)]
+        return small_copy(source, small_in.at[v], m, (back_send, back_recv))
+
+    def small_back_start(m, _):
+        small_back(m).start()
+        return 0
+
+    lax.fori_loop(1, PLACES, small_back_start, 0)
+    small_in[v] = small_in[PLACES + lax.div(v, 4)]
+
     mix_core(w_mo, r_mo_c, mo_r, False)
     mi_flat = w_mi[...].reshape(width, wide)
     sent(o_swap)
     o_send[...] = nt(dps[1 - x], mi_flat).astype(BF16)
     dh1_swap = go(remote(o_send, o_recv, xn))
+    ou_g["a"].wait_recv()
+    add_rows(hs, py, 0, dhp.at[pd, lo])
+    go(ou_g["y0"])
+    ou_g["b"].wait_recv()
+    add_rows(hs, px, half, dhp.at[pd, hi])
+    go(ou_g["x0"])
+    go(ou_g["x1"])
     acc[p] = nt(dps[x], mi_flat)
     w_mi[...] = (
         tn(xs[...].reshape(2 * toks, width), dps[...].reshape(2 * toks, wide))
         .astype(BF16)
         .reshape(w_mi.shape)
     )
-    go(mi_r["core"])
+    go(mi_r["ca"])
+    go(mi_r["cb"])
 
     mix_core(w_mi, r_mi_c, mi_r, True)
-    ou_b.wait_recv()
-
-    def far_part(at):
-        hs[px, at, :] = (hs[px, at, :].astype(F32) + dhp[pd, at, :].astype(F32)).astype(BF16)
-
-    loop(toks, far_part)
-    gu_sum_z1(1)
-    gu_return(0)
-    gu_return(1)
-    go(ou_x)
 
     dn_r["z0"].wait_recv()
     for a in range(2):
         w_dn[a, z0, c] = plus(w_dn[a, z0, c], r_dn_0[a])
     go(dn_r["z1"])
 
+    def mo_idx(a, b):
+        return (a, b, y, c)
+
+    def mi_idx(a, b):
+        return (a, b, y, every, c)
+
+    mo_parts = (w_mo, mo_idx, mo_r, r_mo_y, r_mo_0)
+    mi_parts = (w_mi, mi_idx, mi_r, r_mi_y, r_mi_0)
+
+    def mix_three(w, idx, g, r_y, r_0):
+        g["y3"].wait_recv()
+        at = idx(1 - z1, 1 - z0)
+        w[at] = plus(w[at], r_y[1 - z1, 1 - z0])
+        go(g["s3"])
+
+    def mix_one(w, idx, g, r_y, r_0):
+        g["y1"].wait_recv()
+        g["s3"].wait_recv()
+        at = idx(1 - z1, z0)
+        w[at] = plus(plus(w[at], r_y[1 - z1, z0]), r_0[1 - z1])
+        go(g["s1"])
+
+    def mix_two(w, idx, g, r_y, r_0):
+        g["y2"].wait_recv()
+        at = idx(z1, 1 - z0)
+        w[at] = plus(w[at], r_y[z1, 1 - z0])
+        go(g["s2"])
+
+    def mix_last(w, idx, g, r_y, r_0):
+        g["y0"].wait_recv()
+        g["s2"].wait_recv()
+        at = idx(z1, z0)
+        w[at] = plus(plus(w[at], r_y[z1, z0]), r_0[z1])
+
+    mix_three(*mo_parts)
+    mix_three(*mi_parts)
+    gu_sum_z1(1)
+    gu_return(1)
     dh1_swap.wait_recv()
 
     def norm_one(at):
@@ -828,7 +916,6 @@
         values = tokens[at, :].astype(F32)
         inverse = inverse_rms(values)
         normed = values * inverse
-        small_grad[0:1, :] += jnp.sum(dh * normed, axis=0, keepdims=True)
         q = dh * g1
         input_grad[at, :] = input_grad[at, :] + inverse * (
             q - normed * jnp.mean(q * normed, axis=1, keepdims=True)
@@ -836,53 +923,23 @@
 
     loop(toks, norm_one)
 
-    for q in range(8):
-        small_in[PLACES + q] = small_grad[:, 128 * q : 128 * q + 128]
-
-    def small_back(m):
-        target = lax.rem(v + m, PLACES)
-        source = small_in.at[PLACES + lax.div(target, 4)]
-        return small_copy(source, small_in.at[v], m, (back_send, back_recv))
-
-    def small_back_start(m, _):
-        small_back(m).start()
-        return 0
-
-    lax.fori_loop(1, PLACES, small_back_start, 0)
-    small_in[v] = small_in[PLACES + lax.div(v, 4)]
-
-    def mo_idx(a, b):
-        return (a, b, y, c)
-
-    def mi_idx(a, b):
-        return (a, b, y, every, c)
-
-    def mix_rest(w, idx, g, r_y, r_0, r_1):
-        def add(a, b, other):
-            w[idx(a, b)] = plus(w[idx(a, b)], other)
-
-        g["y3"].wait_recv()
-        add(1 - z1, 1 - z0, r_y[1 - z1, 1 - z0])
-        go(g["s3"])
-        g["y1"].wait_recv()
-        add(1 - z1, z0, r_y[1 - z1, z0])
-        g["s3"].wait_recv()
-        add(1 - z1, z0, r_0[1 - z1])
-        go(g["s1"])
-        g["y2"].wait_recv()
-        add(z1, 1 - z0, r_y[z1, 1 - z0])
-        go(g["s2"])
-        g["y0"].wait_recv()
-        add(z1, z0, r_y[z1, z0])
-        g["s2"].wait_recv()
-        add(z1, z0, r_0[z1])
-
-    mix_rest(w_mo, mo_idx, mo_r, r_mo_y, r_mo_0, r_mo_1)
+    stores = []
+
+    def store(src, dst):
+        copy = pltpu.make_async_copy(src, dst, store_sem.at[len(stores)])
+        copy.start()
+        stores.append(copy)
+
+    store(input_grad, input_sum)
+
+    mix_one(*mo_parts)
+    mix_one(*mi_parts)
+    mix_two(*mo_parts)
+    mix_two(*mi_parts)
     gu_sum_z1(2)
     gu_return(2)
-    mix_rest(w_mi, mi_idx, mi_r, r_mi_y, r_mi_0, r_mi_1)
-    ou_x.wait_recv()
-    ou_y.wait_recv()
+    for name in ("x0", "x1", "y0", "y1"):
+        ou_g[name].wait_recv()
 
     def out_body(at):
         o_send[at, :] = (
@@ -895,42 +952,37 @@
     sent(dh1_swap)
     loop(toks, out_body)
 
-    stores = []
-
-    def store(src, dst):
-        copy = pltpu.make_async_copy(src, dst, store_sem.at[len(stores)])
-        copy.start()
-        stores.append(copy)
-
     store(o_send, block_out)
     down_rows = w_dn.shape[3]
+    def small_back_wait(m, _):
+        small_back(m).wait()
+        return 0
+
+    lax.fori_loop(1, PLACES, small_back_wait, 0)
+    total = small_in[0]
+    for q in range(1, PLACES):
+        total = total + small_in[q]
+    total = total * factor
+    small_out[...] = total
+
+    mix_last(*mo_parts)
     dn_r["z1"].wait_recv()
     acc[3, 0:down_rows] = (w_dn[z1, z0, c].astype(F32) + r_dn_1[...].astype(F32)) * factor
     store(acc.at[3, pl.ds(0, down_rows)], dn_sum)
     mo_r["s1"].wait_recv()
     acc[2, 96 : 96 + rows] = (w_mo[z1, z0, y, c].astype(F32) + r_mo_1[...].astype(F32)) * factor
     store(acc.at[2, pl.ds(96, rows)], mo_sum)
+    for copy in gu_back:
+        copy.wait_recv()
+    store(gu_stage, gu_sum)
+    mix_last(*mi_parts)
     mi_r["s1"].wait_recv()
     w_mi[z1, z0, y, :, c] = plus(w_mi[z1, z0, y, :, c], r_mi_1[...])
     mi_stage[x] = w_mi[z1, z0, y, x, c]
     mi_back = go(remote(w_mi.at[z1, z0, y, 1 - x, c], mi_stage.at[x], xn))
 
-    for copy in gu_back:
-        copy.wait_recv()
-    store(gu_stage, gu_sum)
     mi_back.wait_recv()
     store(mi_stage, mi_sum)
-
-    def small_back_wait(m, _):
-        small_back(m).wait()
-        return 0
-
-    lax.fori_loop(1, PLACES, small_back_wait, 0)
-    total = small_in[0]
-    for q in range(1, PLACES):
-        total = total + small_in[q]
-    total = total * factor
-    small_out[...] = total
 
     for copy in stores:
         copy.wait()
@@ -952,6 +1004,8 @@
     mo_sum,
     gu_sum,
     dn_sum,
+    mixer_in,
+    gain_one,
     block_out,
     input_grad,
     gain_one_grad,
@@ -982,21 +1036,30 @@
             [pieces[q % 4][:, run * (q // 4) : run * (q // 4) + run] for q in range(16)], axis=1
         )
     low = lax.broadcasted_iota(jnp.int32, (rows, 128), 1) < 64
+    by_row = jnp.zeros((rows, 128), F32)
     for b in range(3):
         for q in range(width // 256):
             at = b * half_width + 128 * q
             first = mi_sum[0, :, at : at + 128].astype(F32) * factor
             second = mi_sum[1, :, at : at + 128].astype(F32) * factor
             to = b * width + 256 * q
-            mixer_in_grad[:, to : to + 128] = jnp.where(low, first, pltpu.roll(second, 64, 1))
-            mixer_in_grad[:, to + 128 : to + 256] = jnp.where(low, pltpu.roll(first, 64, 1), second)
+            even = jnp.where(low, first, pltpu.roll(second, 64, 1))
+            odd = jnp.where(low, pltpu.roll(first, 64, 1), second)
+            mixer_in_grad[:, to : to + 128] = even
+            mixer_in_grad[:, to + 128 : to + 256] = odd
+            by_row += even * mixer_in[:, to : to + 128].astype(F32)
+            by_row += odd * mixer_in[:, to + 128 : to + 256].astype(F32)
+    column = jnp.sum(by_row, axis=1, keepdims=True)
+    row_at = lax.broadcasted_iota(jnp.int32, (rows, rows), 0)
+    col_at = lax.broadcasted_iota(jnp.int32, (rows, rows), 1)
+    turned = jnp.sum(jnp.where(row_at == col_at, column, 0.0), axis=0, keepdims=True)
     number = lax.axis_index("dp") * fsdp_count + lax.axis_index("fsdp")
     quarter = lax.rem(lax.div(number, copies_of_place), 4)
     values = small[...]
     own = values[:, 0:rows]
     for k in range(1, 4):
         own = jnp.where(quarter == k, values[:, k * rows : k * rows + rows], own)
-    gain_one_grad[...] = own[0:1]
+    gain_one_grad[...] = turned / gain_one[...].astype(F32)
     gain_two_grad[...] = own[1:2]
     taps_grad[...] = own[2:5]
 
@@ -1045,6 +1108,11 @@
 
     half = toks // 2
     scratch = [
+        vm((toks, width), F32),
+        vm((toks, width)),
+        vm((rows, 3 * width)),
+        vm((rows, ff)),
+        vm((rows, ff)),
         vm((8, 128), F32),
         vm((PLACES, 8, 128), F32),
         vm((8, width), F32),
@@ -1095,7 +1163,7 @@
         vm((8, width + half_width), F32),
         pltpu.SemaphoreType.DMA((COPIES,)),
         pltpu.SemaphoreType.DMA((COPIES,)),
-        pltpu.SemaphoreType.DMA((3,)),
+        pltpu.SemaphoreType.DMA((7,)),
         pltpu.SemaphoreType.DMA((20,)),
         pltpu.SemaphoreType.DMA((PLACES,)),
         pltpu.SemaphoreType.DMA((PLACES,)),
@@ -1118,8 +1186,8 @@
     result = pl.pallas_call(
         functools.partial(kernel, fsdp_count, spare, factor),
         out_shape=outs,
-        in_specs=[vmem, hbm] + [vmem] * 6 + [hbm] + [vmem] * 2 + [hbm],
-        out_specs=[hbm] + [vmem] * 2 + [hbm] * 4,
+        in_specs=[hbm] * 2 + [vmem] * 5 + [hbm] * 5,
+        out_specs=[hbm] * 2 + [vmem] + [hbm] * 4,
         scratch_shapes=scratch,
         compiler_params=pltpu.CompilerParams(
             collective_id=0, has_side_effects=True, vmem_limit_bytes=60 << 20
@@ -1152,10 +1220,10 @@
             jax.ShapeDtypeStruct((rows, ff), F32),
             jax.ShapeDtypeStruct((down_rows, width), F32),
         ],
-        in_specs=[vmem] * 7,
+        in_specs=[vmem] * 9,
         out_specs=[vmem] * 10,
         compiler_params=pltpu.CompilerParams(vmem_limit_bytes=60 << 20),
-    )(*result)
+    )(*result, mixer_in, first_gain.reshape(1, rows))
     block_out, input_grad, g_one, g_mi, g_taps, g_mo, g_two, g_gate, g_up, g_down = finished
 
     def shared(item, axis=0):

time: 207 us -> 198 us (0.957)
  Pallas kernels: 206 us -> 197 us
    pallas_call x1, Pallas kernels: 202 us -> 193 us  [per_device(): pl.pallas_call(functools.partial(kernel, fsdp_count, spare, factor), out_...]
where the time goes in v3:
time: 198 us
  Pallas kernels  197 us (99%)
    pallas_call x1, Pallas kernels, per_device(): pl.pallas_call(functools.partial(kernel, fsdp_count, spare, factor), out_...  193 us
    pallas_call x1, Pallas kernels, per_device(): pl.pallas_call(functools.partial(finish, fsdp_count, spare, factor), out_...  4.34 us

profile of v3, /device:TPU:0, one launch (start us, length us, event | category | flops | bytes accessed | tf_op | source)
XLA Modules:
  0.0 197.7 jit_solution(2000447779234786794)
XLA Ops:
  0.6 192.7 %shard_map.195 = (bf16[256,1024]{1,0:T(8,128)(2,1)}, f32[256,1024]{1,0:T(8,128)}, f32[8,128]{1,0:T(8,128)}, bf16[2,32,1536]{2,1,0:T(8,128)(2,1)}, f32[32,1024]{1...) custom-call(bf16[256,1024]{1,0:T(8,128)(2,1)} %bitcast.8, bf16[256,1024]{1,0:T(8,128)(2,1)} %bitcast.9, ...), custom_call_target="tpu_custom_call" | custom-call | tf_op jit(solution)/shard_map/pallas_call | solution.py:1186
  193.4 4.3 %shard_map.196 = (bf16[256,1024]{1,0:T(8,128)(2,1)}, f32[256,1024]{1,0:T(8,128)}, f32[1,32]{1,0:T(1,128)}, f32[32,3072]{1,0:T(8,128)}, f32[3,32]{1,0:T(4,128)}, ...) custom-call(bf16[256,1024]{1,0:T(8,128)(2,1)} %get-tuple-element.27., ...), custom_call_target="tpu_custom_call" | custom-call | tf_op jit(solution)/shard_map/pallas_call | solution.py:1209

commit v4 on v3

--- a/solution.py
+++ b/solution.py
@@ -271,6 +271,9 @@
 
     mo_g = mix_gather(mo_at)
     mi_gs = [mix_gather(mi_half(0)), mix_gather(mi_half(1))]
+    load_out.wait()
+    go(mo_g["s1"])
+    go(mo_g["s2"])
     mi_swap.wait_recv()
     for g in mi_gs:
         for name in ("s1", "s2", "y0"):
@@ -374,12 +377,12 @@
     for j in range(3):
         w_gu[j, z1, z0, p, c] = gu_stage[p, j]
 
+    go(mo_g["y0"])
+    forward(mo_g, "s1", ("s3", "y1"))
+    forward(mo_g, "s2", ("y2",))
     for g in mi_gs:
         forward(g, "s1", ("s3", "y1"))
         forward(g, "s2", ("y2",))
-    load_out.wait()
-    go(mo_g["s1"])
-    go(mo_g["s2"])
     gu_swap = [
         remote(gu_stage.at[px], w_gu.at[:, z1, z0, p, c], xn),
         remote(gu_stage.at[py], w_gu.at[:, z1, z0, p, c], yn),
@@ -436,17 +439,14 @@
     for g in mi_gs:
         forward(g, "s3", ("y3",))
         go(g["ca"])
+    forward(mo_g, "s3", ("y3",))
+    go(mo_g["ca"])
     go(gu_swap[1])
-    go(mo_g["y0"])
-    forward(mo_g, "s1", ("s3", "y1"))
     load_down.wait()
     z_start(dn_g)
     hidden_one(x)
     tok_swap.wait_recv()
     hidden_one(1 - x)
-    forward(mo_g, "s2", ("y2",))
-    forward(mo_g, "s3", ("y3",))
-    go(mo_g["ca"])
     for g in mi_gs:
         for name in ("y0", "y1", "y2", "y3"):
             g[name].wait_recv()
@@ -545,12 +545,18 @@
             sg = jax.nn.sigmoid(a)
             silu = a * sg
             ms[slot, inner, j * part : j * part + part] = (silu * b).astype(BF16)
-            dabs[j, slot, inner, 0:part] = (d * b * sg * (1.0 + a * (1.0 - sg))).astype(BF16)
-            dabs[j, slot, inner, part:] = (d * silu).astype(BF16)
+            chunk = lax.rem(i, toks // step)
+            at = (lax.div(chunk, 4), lax.rem(lax.div(chunk, 2), 2), lax.rem(chunk, 2))
+            dabs[(j, lax.div(base, 2), which, *at, every, slice(0, part))] = (
+                d * b * sg * (1.0 + a * (1.0 - sg))
+            ).astype(BF16)
+            dabs[(j, lax.div(base, 2), which, *at, every, slice(part, 2 * part))] = (
+                d * silu
+            ).astype(BF16)
             return 0
 
         lax.fori_loop(0, 2 * toks // step, body, 0)
-        back = nt(dabs[j, pl.ds(base, 2)].reshape(2 * toks, 2 * part), w)
+        back = nt(dabs[j, lax.div(base, 2)].reshape(2 * toks, 2 * part), w)
         back = back.reshape(2, toks, width)
         if j == 0:
             acc[pl.ds(base, 2)] = back
@@ -645,17 +651,17 @@
     gu_g[0]["core"].wait_recv()
     feed(0, ya)
     z_core(gu_g[1])
-    z_forward(gu_g[2])
     plane_pair(gs_g, ("y0", "y1", "fx"))
     plane_pair(hs_g, ("y0", "fx", "fy"))
     feed(0, yb)
     gathered(gu_g[0])
     gu_weight_grad(0)
     go(gu_r[0]["core"])
-    z_core(gu_g[2])
+    z_forward(gu_g[2])
     gu_g[1]["core"].wait_recv()
     feed(1, yb)
     gu_after_core(0)
+    z_core(gu_g[2])
     feed(1, ya)
     gu_g[2]["core"].wait_recv()
     feed(2, yb)
@@ -663,9 +669,9 @@
     go(dh_g["a"])
     go(dh_g["b"])
     go(dh_g["y1"])
+    gu_after_z0(0)
     feed(2, ya)
     go(dh_g["x0"])
-    gu_after_z0(0)
     gathered(gu_g[1])
     gu_weight_grad(1)
     go(gu_r[1]["core"])
@@ -740,6 +746,7 @@
     gu_after_z0(1)
     gu_sum_z1(0)
     gu_return(0)
+    gu_after_z0(2)
     do_swap.wait_recv()
     dkbuf[1 - x, 0:toks, 0:half_width] = nt(dos[1 - x], mo_flat)
     split_dy(1 - x)
@@ -773,11 +780,15 @@
         )
 
     mo_r = mix_reduce(mo_at, r_mo_c, r_mo_y, r_mo_0, r_mo_1)
-    mi_r = mix_reduce(mi_at, r_mi_c, r_mi_y, r_mi_0, r_mi_1)
+    mi_rs = [
+        mix_reduce(
+            lambda a, b, yy, cc, h=h: dabs.at[h, a, b, yy, :, cc],
+            r_mi_c.at[h], r_mi_y.at[h], r_mi_0.at[h], r_mi_1.at[h],
+        )
+        for h in range(2)
+    ]
     go(mo_r["ca"])
     go(mo_r["cb"])
-    gu_after_z0(2)
-
     def mix_core(w, r_c, g, with_x):
         def add(yy):
             for a in range(2):
@@ -844,10 +855,24 @@
     small_in[v] = small_in[PLACES + lax.div(v, 4)]
 
     mix_core(w_mo, r_mo_c, mo_r, False)
+    columns = 2 * part
+    for h in range(2):
+        dabs[h] = (
+            tn(
+                xs[...].reshape(2 * toks, width),
+                dps[:, :, h * columns : (h + 1) * columns].reshape(2 * toks, columns),
+            )
+            .astype(BF16)
+            .reshape(dabs.shape[1:])
+        )
+        go(mi_rs[h]["ca"])
+        go(mi_rs[h]["cb"])
     mi_flat = w_mi[...].reshape(width, wide)
     sent(o_swap)
     o_send[...] = nt(dps[1 - x], mi_flat).astype(BF16)
     dh1_swap = go(remote(o_send, o_recv, xn))
+    mix_core(dabs.at[0], r_mi_c.at[0], mi_rs[0], True)
+    mix_core(dabs.at[1], r_mi_c.at[1], mi_rs[1], True)
     ou_g["a"].wait_recv()
     add_rows(hs, py, 0, dhp.at[pd, lo])
     go(ou_g["y0"])
@@ -855,21 +880,11 @@
     add_rows(hs, px, half, dhp.at[pd, hi])
     go(ou_g["x0"])
     go(ou_g["x1"])
-    acc[p] = nt(dps[x], mi_flat)
-    w_mi[...] = (
-        tn(xs[...].reshape(2 * toks, width), dps[...].reshape(2 * toks, wide))
-        .astype(BF16)
-        .reshape(w_mi.shape)
-    )
-    go(mi_r["ca"])
-    go(mi_r["cb"])
-
-    mix_core(w_mi, r_mi_c, mi_r, True)
-
     dn_r["z0"].wait_recv()
     for a in range(2):
         w_dn[a, z0, c] = plus(w_dn[a, z0, c], r_dn_0[a])
     go(dn_r["z1"])
+    acc[p] = nt(dps[x], mi_flat)
 
     def mo_idx(a, b):
         return (a, b, y, c)
@@ -878,7 +893,9 @@
         return (a, b, y, every, c)
 
     mo_parts = (w_mo, mo_idx, mo_r, r_mo_y, r_mo_0)
-    mi_parts = (w_mi, mi_idx, mi_r, r_mi_y, r_mi_0)
+    mi_parts = [
+        (dabs.at[h], mi_idx, mi_rs[h], r_mi_y.at[h], r_mi_0.at[h]) for h in range(2)
+    ]
 
     def mix_three(w, idx, g, r_y, r_0):
         g["y3"].wait_recv()
@@ -906,7 +923,8 @@
         w[at] = plus(plus(w[at], r_y[z1, z0]), r_0[z1])
 
     mix_three(*mo_parts)
-    mix_three(*mi_parts)
+    mix_three(*mi_parts[0])
+    mix_three(*mi_parts[1])
     gu_sum_z1(1)
     gu_return(1)
     dh1_swap.wait_recv()
@@ -933,9 +951,11 @@
     store(input_grad, input_sum)
 
     mix_one(*mo_parts)
-    mix_one(*mi_parts)
+    mix_one(*mi_parts[0])
+    mix_one(*mi_parts[1])
     mix_two(*mo_parts)
-    mix_two(*mi_parts)
+    mix_two(*mi_parts[0])
+    mix_two(*mi_parts[1])
     gu_sum_z1(2)
     gu_return(2)
     for name in ("x0", "x1", "y0", "y1"):
@@ -975,13 +995,16 @@
     for copy in gu_back:
         copy.wait_recv()
     store(gu_stage, gu_sum)
-    mix_last(*mi_parts)
-    mi_r["s1"].wait_recv()
-    w_mi[z1, z0, y, :, c] = plus(w_mi[z1, z0, y, :, c], r_mi_1[...])
-    mi_stage[x] = w_mi[z1, z0, y, x, c]
-    mi_back = go(remote(w_mi.at[z1, z0, y, 1 - x, c], mi_stage.at[x], xn))
-
-    mi_back.wait_recv()
+    mi_back = []
+    for h in range(2):
+        mix_last(*mi_parts[h])
+        mi_rs[h]["s1"].wait_recv()
+        dabs[h, z1, z0, y, :, c] = plus(dabs[h, z1, z0, y, :, c], r_mi_1[h])
+        into = pl.ds(h * columns, columns)
+        mi_stage[x, :, into] = dabs[h, z1, z0, y, x, c]
+        mi_back.append(go(remote(dabs.at[h, z1, z0, y, 1 - x, c], mi_stage.at[x, :, into], xn)))
+    for copy in mi_back:
+        copy.wait_recv()
     store(mi_stage, mi_sum)
 
     for copy in stores:
@@ -1138,7 +1161,7 @@
         vm((2, toks + 8, 2 * part), F32),
         vm((2 * toks, part), F32),
         vm((4, toks, 3 * part)),
-        vm((3, 4, toks, 2 * part)),
+        vm((3, 2, 2, 2, 2, 2, rows, 2 * part)),
         vm((4, toks, width), F32),
         vm((4, toks, width)),
         vm((half, width)),
@@ -1152,10 +1175,10 @@
         vm((2, 2, down_rows, width)),
         vm((2, down_rows, width)),
         vm((down_rows, width)),
-        vm((2, 2, 2, 2, rows, wide)),
-        vm((2, 2, 2, rows, wide)),
-        vm((2, 2, rows, wide)),
-        vm((2, rows, wide)),
+        vm((2, 2, 2, 2, 2, rows, 2 * part)),
+        vm((2, 2, 2, 2, rows, 2 * part)),
+        vm((2, 2, 2, rows, 2 * part)),
+        vm((2, 2, rows, 2 * part)),
         vm((2, 2, 2, rows, width)),
         vm((2, 2, rows, width)),
         vm((2, rows, width)),

time: 198 us -> 193 us (0.975)
  Pallas kernels: 197 us -> 192 us
    pallas_call x1, Pallas kernels: 193 us -> 187 us  [per_device(): pl.pallas_call(functools.partial(kernel, fsdp_count, spare, factor), out_...]
where the time goes in v4:
time: 193 us; the launch traced here: 192 us
  Pallas kernels  192 us (99%)
    pallas_call x1, Pallas kernels, per_device(): pl.pallas_call(functools.partial(kernel, fsdp_count, spare, factor), out_...  187 us
    pallas_call x1, Pallas kernels, per_device(): pl.pallas_call(functools.partial(finish, fsdp_count, spare, factor), out_...  4.34 us

profile of v4, /device:TPU:0, one launch (start us, length us, event | category | flops | bytes accessed | tf_op | source)
XLA Modules:
  0.0 192.4 jit_solution(11618815635984202197)
XLA Ops:
  0.6 187.4 %shard_map.195 = (bf16[256,1024]{1,0:T(8,128)(2,1)}, f32[256,1024]{1,0:T(8,128)}, f32[8,128]{1,0:T(8,128)}, bf16[2,32,1536]{2,1,0:T(8,128)(2,1)}, f32[32,1024]{1...) custom-call(bf16[256,1024]{1,0:T(8,128)(2,1)} %bitcast.8, bf16[256,1024]{1,0:T(8,128)(2,1)} %bitcast.9, ...), custom_call_target="tpu_custom_call" | custom-call | tf_op jit(solution)/shard_map/pallas_call | solution.py:1209
  188.1 4.3 %shard_map.196 = (bf16[256,1024]{1,0:T(8,128)(2,1)}, f32[256,1024]{1,0:T(8,128)}, f32[1,32]{1,0:T(1,128)}, f32[32,3072]{1,0:T(8,128)}, f32[3,32]{1,0:T(4,128)}, ...) custom-call(bf16[256,1024]{1,0:T(8,128)(2,1)} %get-tuple-element.27., ...), custom_call_target="tpu_custom_call" | custom-call | tf_op jit(solution)/shard_map/pallas_call | solution.py:1232

commit v5 on v4

--- a/solution.py
+++ b/solution.py
@@ -654,13 +654,13 @@
     plane_pair(gs_g, ("y0", "y1", "fx"))
     plane_pair(hs_g, ("y0", "fx", "fy"))
     feed(0, yb)
+    z_forward(gu_g[2])
     gathered(gu_g[0])
     gu_weight_grad(0)
     go(gu_r[0]["core"])
-    z_forward(gu_g[2])
+    gu_after_core(0)
     gu_g[1]["core"].wait_recv()
     feed(1, yb)
-    gu_after_core(0)
     z_core(gu_g[2])
     feed(1, ya)
     gu_g[2]["core"].wait_recv()

time: 193 us -> 191 us (0.990)
  Pallas kernels: 192 us -> 190 us
where the time goes in v5:
time: 191 us
  Pallas kernels  190 us (99%)
    pallas_call x1, Pallas kernels, per_device(): pl.pallas_call(functools.partial(kernel, fsdp_count, spare, factor), out_...  186 us
    pallas_call x1, Pallas kernels, per_device(): pl.pallas_call(functools.partial(finish, fsdp_count, spare, factor), out_...  4.34 us

profile of v5, /device:TPU:0, one launch (start us, length us, event | category | flops | bytes accessed | tf_op | source)
XLA Modules:
  0.0 190.8 jit_solution(10022826704930151090)
XLA Ops:
  0.6 185.8 %shard_map.195 = (bf16[256,1024]{1,0:T(8,128)(2,1)}, f32[256,1024]{1,0:T(8,128)}, f32[8,128]{1,0:T(8,128)}, bf16[2,32,1536]{2,1,0:T(8,128)(2,1)}, f32[32,1024]{1...) custom-call(bf16[256,1024]{1,0:T(8,128)(2,1)} %bitcast.8, bf16[256,1024]{1,0:T(8,128)(2,1)} %bitcast.9, ...), custom_call_target="tpu_custom_call" | custom-call | tf_op jit(solution)/shard_map/pallas_call | solution.py:1209
  186.4 4.3 %shard_map.196 = (bf16[256,1024]{1,0:T(8,128)(2,1)}, f32[256,1024]{1,0:T(8,128)}, f32[1,32]{1,0:T(1,128)}, f32[32,3072]{1,0:T(8,128)}, f32[3,32]{1,0:T(4,128)}, ...) custom-call(bf16[256,1024]{1,0:T(8,128)(2,1)} %get-tuple-element.27., ...), custom_call_target="tpu_custom_call" | custom-call | tf_op jit(solution)/shard_map/pallas_call | solution.py:1232

commit v6 on v5

--- a/solution.py
+++ b/solution.py
@@ -873,6 +873,10 @@
     dh1_swap = go(remote(o_send, o_recv, xn))
     mix_core(dabs.at[0], r_mi_c.at[0], mi_rs[0], True)
     mix_core(dabs.at[1], r_mi_c.at[1], mi_rs[1], True)
+    dn_r["z0"].wait_recv()
+    for a in range(2):
+        w_dn[a, z0, c] = plus(w_dn[a, z0, c], r_dn_0[a])
+    go(dn_r["z1"])
     ou_g["a"].wait_recv()
     add_rows(hs, py, 0, dhp.at[pd, lo])
     go(ou_g["y0"])
@@ -880,10 +884,6 @@
     add_rows(hs, px, half, dhp.at[pd, hi])
     go(ou_g["x0"])
     go(ou_g["x1"])
-    dn_r["z0"].wait_recv()
-    for a in range(2):
-        w_dn[a, z0, c] = plus(w_dn[a, z0, c], r_dn_0[a])
-    go(dn_r["z1"])
     acc[p] = nt(dps[x], mi_flat)
 
     def mo_idx(a, b):
@@ -925,8 +925,6 @@
     mix_three(*mo_parts)
     mix_three(*mi_parts[0])
     mix_three(*mi_parts[1])
-    gu_sum_z1(1)
-    gu_return(1)
     dh1_swap.wait_recv()
 
     def norm_one(at):
@@ -949,12 +947,14 @@
         stores.append(copy)
 
     store(input_grad, input_sum)
+    gu_sum_z1(1)
+    gu_return(1)
 
     mix_one(*mo_parts)
+    mix_two(*mo_parts)
     mix_one(*mi_parts[0])
+    mix_two(*mi_parts[0])
     mix_one(*mi_parts[1])
-    mix_two(*mo_parts)
-    mix_two(*mi_parts[0])
     mix_two(*mi_parts[1])
     gu_sum_z1(2)
     gu_return(2)
@@ -1073,16 +1073,27 @@
             by_row += even * mixer_in[:, to : to + 128].astype(F32)
             by_row += odd * mixer_in[:, to + 128 : to + 256].astype(F32)
     column = jnp.sum(by_row, axis=1, keepdims=True)
-    row_at = lax.broadcasted_iota(jnp.int32, (rows, rows), 0)
-    col_at = lax.broadcasted_iota(jnp.int32, (rows, rows), 1)
+    every_row = gain_one.shape[1]
+    step = pl.program_id(0)
+    row_at = lax.broadcasted_iota(jnp.int32, (rows, every_row), 0) + step * rows
+    col_at = lax.broadcasted_iota(jnp.int32, (rows, every_row), 1)
     turned = jnp.sum(jnp.where(row_at == col_at, column, 0.0), axis=0, keepdims=True)
+    turned = turned / gain_one[...].astype(F32)
     number = lax.axis_index("dp") * fsdp_count + lax.axis_index("fsdp")
     quarter = lax.rem(lax.div(number, copies_of_place), 4)
     values = small[...]
-    own = values[:, 0:rows]
+    own = values[:, 0:every_row]
     for k in range(1, 4):
-        own = jnp.where(quarter == k, values[:, k * rows : k * rows + rows], own)
-    gain_one_grad[...] = turned / gain_one[...].astype(F32)
+        own = jnp.where(quarter == k, values[:, k * every_row : (k + 1) * every_row], own)
+
+    @pl.when(step == 0)
+    def first_step():
+        gain_one_grad[...] = turned
+
+    @pl.when(step > 0)
+    def later_step():
+        gain_one_grad[...] += turned
+
     gain_two_grad[...] = own[1:2]
     taps_grad[...] = own[2:5]
 
@@ -1229,6 +1240,12 @@
         up_weight,
         down_weight,
     )
+    def halved(count, columns):
+        return pl.BlockSpec((count // 2, columns), lambda i: (i, 0))
+
+    def whole(count, columns):
+        return pl.BlockSpec((count, columns), lambda i: (0, 0))
+
     finished = pl.pallas_call(
         functools.partial(finish, fsdp_count, spare, factor),
         out_shape=[
@@ -1243,8 +1260,30 @@
             jax.ShapeDtypeStruct((rows, ff), F32),
             jax.ShapeDtypeStruct((down_rows, width), F32),
         ],
-        in_specs=[vmem] * 9,
-        out_specs=[vmem] * 10,
+        grid=(2,),
+        in_specs=[
+            halved(toks, width),
+            halved(toks, width),
+            whole(8, 128),
+            pl.BlockSpec((2, rows // 2, wide), lambda i: (0, i, 0)),
+            halved(rows, width),
+            pl.BlockSpec((4, 3, rows // 2, 2 * part), lambda i: (0, 0, i, 0)),
+            halved(down_rows, width),
+            halved(rows, 3 * width),
+            whole(1, rows),
+        ],
+        out_specs=[
+            halved(toks, width),
+            halved(toks, width),
+            whole(1, rows),
+            halved(rows, 3 * width),
+            whole(3, rows),
+            halved(rows, width),
+            whole(1, rows),
+            halved(rows, ff),
+            halved(rows, ff),
+            halved(down_rows, width),
+        ],
         compiler_params=pltpu.CompilerParams(vmem_limit_bytes=60 << 20),
     )(*result, mixer_in, first_gain.reshape(1, rows))
     block_out, input_grad, g_one, g_mi, g_taps, g_mo, g_two, g_gate, g_up, g_down = finished

time: 191 us -> 191 us (level)
  no operation moved by 1% of the time
where the time goes in v6:
time: 191 us; the launch traced here: 190 us
  Pallas kernels  190 us (99%)
    pallas_call x1, Pallas kernels, per_device(): pl.pallas_call(functools.partial(kernel, fsdp_count, spare, factor), out_...  186 us

profile of v6, /device:TPU:0, one launch (start us, length us, event | category | flops | bytes accessed | tf_op | source)
XLA Modules:
  0.0 190.4 jit_solution(13146656430628000933)
XLA Ops:
  0.6 185.8 %shard_map.195 = (bf16[256,1024]{1,0:T(8,128)(2,1)}, f32[256,1024]{1,0:T(8,128)}, f32[8,128]{1,0:T(8,128)}, bf16[2,32,1536]{2,1,0:T(8,128)(2,1)}, f32[32,1024]{1...) custom-call(bf16[256,1024]{1,0:T(8,128)(2,1)} %bitcast.8, bf16[256,1024]{1,0:T(8,128)(2,1)} %bitcast.9, ...), custom_call_target="tpu_custom_call" | custom-call | tf_op jit(solution)/shard_map/pallas_call | solution.py:1220
  186.5 3.7 %shard_map.196 = (bf16[256,1024]{1,0:T(8,128)(2,1)}, f32[256,1024]{1,0:T(8,128)}, f32[1,32]{1,0:T(1,128)}, f32[32,3072]{1,0:T(8,128)}, f32[3,32]{1,0:T(4,128)}, ...) custom-call(bf16[256,1024]{1,0:T(8,128)(2,1)} %get-tuple-element.27., ...), custom_call_target="tpu_custom_call" | custom-call | tf_op jit(solution)/shard_map/pallas_call | solution.py:1249

commit v7 on v6

--- a/solution.py
+++ b/solution.py
@@ -992,9 +992,6 @@
     mo_r["s1"].wait_recv()
     acc[2, 96 : 96 + rows] = (w_mo[z1, z0, y, c].astype(F32) + r_mo_1[...].astype(F32)) * factor
     store(acc.at[2, pl.ds(96, rows)], mo_sum)
-    for copy in gu_back:
-        copy.wait_recv()
-    store(gu_stage, gu_sum)
     mi_back = []
     for h in range(2):
         mix_last(*mi_parts[h])
@@ -1003,6 +1000,9 @@
         into = pl.ds(h * columns, columns)
         mi_stage[x, :, into] = dabs[h, z1, z0, y, x, c]
         mi_back.append(go(remote(dabs.at[h, z1, z0, y, 1 - x, c], mi_stage.at[x, :, into], xn)))
+    for copy in gu_back:
+        copy.wait_recv()
+    store(gu_stage, gu_sum)
     for copy in mi_back:
         copy.wait_recv()
     store(mi_stage, mi_sum)

time: 191 us -> 191 us (level)
  no operation moved by 1% of the time
where the time goes in v7:
time: 191 us; the launch traced here: 190 us
  Pallas kernels  190 us (99%)
    pallas_call x1, Pallas kernels, per_device(): pl.pallas_call(functools.partial(kernel, fsdp_count, spare, factor), out_...  186 us

profile of v7, /device:TPU:0, one launch (start us, length us, event | category | flops | bytes accessed | tf_op | source)
XLA Modules:
  0.0 190.4 jit_solution(18233660494063734061)
XLA Ops:
  0.6 185.8 %shard_map.195 = (bf16[256,1024]{1,0:T(8,128)(2,1)}, f32[256,1024]{1,0:T(8,128)}, f32[8,128]{1,0:T(8,128)}, bf16[2,32,1536]{2,1,0:T(8,128)(2,1)}, f32[32,1024]{1...) custom-call(bf16[256,1024]{1,0:T(8,128)(2,1)} %bitcast.8, bf16[256,1024]{1,0:T(8,128)(2,1)} %bitcast.9, ...), custom_call_target="tpu_custom_call" | custom-call | tf_op jit(solution)/shard_map/pallas_call | solution.py:1220
  186.5 3.7 %shard_map.196 = (bf16[256,1024]{1,0:T(8,128)(2,1)}, f32[256,1024]{1,0:T(8,128)}, f32[1,32]{1,0:T(1,128)}, f32[32,3072]{1,0:T(8,128)}, f32[3,32]{1,0:T(4,128)}, ...) custom-call(bf16[256,1024]{1,0:T(8,128)(2,1)} %get-tuple-element.27., ...), custom_call_target="tpu_custom_call" | custom-call | tf_op jit(solution)/shard_map/pallas_call | solution.py:1249
